TPU v7x, 32 devices: a whole 2x2x4 slice. The times are simulated.
32 devices in a mesh: seq: 4 (over y, x), exp: 8 (over z, core).
Axes of the slice: x: 2, y: 2, z: 4, core: 2. Of those that a mesh axis runs over, the one named last changes fastest.
Arguments:
- query: bfloat16 [512, 1024], P('seq', 'exp'), may hold values from -6 to 6
- key_in: bfloat16 [512, 1024], P('seq', 'exp'), may hold values from -6 to 6
- value: bfloat16 [512, 1024], P('seq', 'exp'), may hold values from -6 to 6
- decay_log: float32 [512, 8], P('seq', 'exp'), may hold values from -1 to 0
- norm_gain: bfloat16 [1024], P('exp'), may hold values from 0.099609375 to 1.8984375
- w_out: bfloat16 [1024, 4096], P('exp'), may hold values from -0.1875 to 0.1875
- router: bfloat16 [4096, 4], replicated, may hold values from -0.09375 to 0.09375
- routes: int32 [512, 2], P('seq'), may hold values from 0 to 3, all different within a row; in each aligned block of 128 rows (0 to 127, 128 to 255, ...) at most 96 rows name the same one
- w_gate: bfloat16 [8, 4096, 288], P('exp'), may hold values from -0.09375 to 0.09375
- w_up: bfloat16 [8, 4096, 288], P('exp'), may hold values from -0.09375 to 0.09375
- w_down: bfloat16 [8, 288, 4096], P('exp'), may hold values from -0.25 to 0.25
Outputs:
- output: bfloat16 [512, 4096], P(('seq', 'exp'))
Inputs may be any that keep to these rules, and one draw needn't show every extreme that they name: `routes`: among the positions of one block of 128 positions no expert is named more than 96 times, a bound that some block reaches; a position names 2 different experts.
All inputs are finite; a program needn't handle non-finite values.
Results may differ from a plain program's by a relative error of at most 0.015.
Values may be sent and summed in bfloat16 or wider, within the bound.
No kernel may reach another device: no remote copies, remote signals or barrier semaphores. Data moves between devices by JAX's collectives and lax.ppermute only.
A program may use at most 64 MiB of HBM per device.

v0:
```python
import jax
import jax.numpy as jnp
from jax import lax
from jax.sharding import PartitionSpec as P


def local(query, key_in, value, decay_log, norm_gain, w_out, router, routes, w_gate, w_up, w_down):
    tok_count = query.shape[0]
    head_count = decay_log.shape[1]
    head_size = query.shape[1] // head_count
    top_count = routes.shape[1]
    expert_count = router.shape[1]
    capacity = max(2, 3 * tok_count * top_count // (2 * expert_count))
    exp_count = lax.axis_size("exp")
    slice_count = exp_count // expert_count
    queries = query.reshape(tok_count, head_count, head_size)
    keys_local = key_in.reshape(tok_count, head_count, head_size)
    values_local = value.reshape(tok_count, head_count, head_size)
    cumulative = jnp.cumsum(decay_log, axis=0)
    scores = jnp.einsum("thd,shd->hts", queries, keys_local, preferred_element_type=jnp.float32)
    spread = cumulative.T[:, :, None] - cumulative.T[:, None, :]
    causal = jnp.arange(tok_count)[:, None] >= jnp.arange(tok_count)[None, :]
    weights = jnp.where(causal, jnp.exp(jnp.where(causal, spread, 0.0)), 0.0)
    attend = (scores * weights / head_size).astype(jnp.bfloat16)
    intra_part = jnp.einsum(
        "hts,she->the", attend, values_local, preferred_element_type=jnp.float32
    )
    totals = cumulative[-1]
    tail_decay = jnp.exp(totals[None, :] - cumulative)
    state_delta = jnp.einsum(
        "shd,she->hde",
        keys_local.astype(jnp.float32) * tail_decay[:, :, None],
        values_local.astype(jnp.float32),
        precision=lax.Precision.HIGHEST,
    )
    decay_rows = lax.all_gather(totals[None, :], "seq", axis=0, tiled=True)
    my_rank = lax.axis_index("seq")
    seq_ranks = jnp.arange(decay_rows.shape[0])
    state_piece = lax.all_gather(
        state_delta[None].astype(jnp.bfloat16), "seq", axis=0, tiled=True
    ).astype(jnp.float32)
    piece_rank = jnp.arange(state_piece.shape[0])
    between = (seq_ranks[None, :] > piece_rank[:, None]) & (seq_ranks[None, :] < my_rank)
    logsum = jnp.dot(between.astype(jnp.float32), decay_rows, precision=lax.Precision.HIGHEST)
    factor = jnp.where((piece_rank < my_rank)[:, None], jnp.exp(logsum), 0.0)
    incoming = jnp.zeros_like(state_delta) + jnp.einsum(
        "ih,ihde->hde", factor, state_piece, precision=lax.Precision.HIGHEST
    )
    inter_part = (
        jnp.exp(cumulative)[:, :, None]
        * jnp.einsum(
            "thd,hde->the", queries.astype(jnp.float32), incoming, precision=lax.Precision.HIGHEST
        )
        / head_size
    )
    attended = intra_part + inter_part
    inverse_rms = lax.rsqrt(jnp.mean(attended * attended, axis=-1, keepdims=True) + 1e-06)
    gain_f32 = norm_gain.astype(jnp.float32).reshape(head_count, head_size)
    normed = (
        (attended * inverse_rms * gain_f32)
        .astype(jnp.bfloat16)
        .reshape(tok_count, head_count * head_size)
    )
    own_mixed = lax.psum_scatter(
        jnp.dot(normed, w_out, preferred_element_type=jnp.float32),
        "exp",
        scatter_dimension=0,
        tiled=True,
    ).astype(jnp.bfloat16)
    mixed = lax.all_gather(own_mixed, "exp", axis=0, tiled=True)
    logits = jnp.dot(mixed, router, preferred_element_type=jnp.float32)
    member = routes[:, :, None] == jnp.arange(expert_count)[None, None, :]
    picked = jnp.sum(jnp.where(member, logits[:, None, :], 0.0), axis=-1)
    raised = jnp.exp(picked)
    gate_probs = raised / jnp.sum(raised, axis=-1, keepdims=True)
    my_expert = lax.axis_index("exp") // slice_count
    flat_hit = (routes.reshape(-1) == my_expert).astype(jnp.int32)
    slot_flat = jnp.cumsum(flat_hit) - flat_hit
    slot_match = (slot_flat[:, None] == jnp.arange(capacity)[None, :]) & (flat_hit[:, None] > 0)
    token_select = jnp.sum(
        slot_match.reshape(tok_count, top_count, capacity).astype(jnp.float32), axis=1
    )
    token_gate = jnp.sum(jnp.where(routes == my_expert, gate_probs, 0.0), axis=1)
    slot_rows = jnp.dot(
        token_select.astype(jnp.bfloat16).T, mixed, preferred_element_type=jnp.float32
    ).astype(jnp.bfloat16)
    gate_part = jnp.dot(slot_rows, w_gate[0], preferred_element_type=jnp.float32)
    up_part = jnp.dot(slot_rows, w_up[0], preferred_element_type=jnp.float32)
    hidden = (jax.nn.silu(gate_part) * up_part).astype(jnp.bfloat16)
    slice_out = jnp.dot(hidden, w_down[0], preferred_element_type=jnp.float32)
    spread_out = jnp.dot(token_select, slice_out, precision=lax.Precision.HIGHEST)
    summed = lax.psum_scatter(
        token_gate[:, None] * spread_out, "exp", scatter_dimension=0, tiled=True
    )
    return (own_mixed.astype(jnp.float32) + summed).astype(jnp.bfloat16)


def solution(mesh):
    placed = (
        P("seq", "exp"),
        P("seq", "exp"),
        P("seq", "exp"),
        P("seq", "exp"),
        P("exp"),
        P("exp", None),
        P(),
        P("seq", None),
        P("exp", None, None),
        P("exp", None, None),
        P("exp", None, None),
    )
    return jax.shard_map(
        local, mesh=mesh, in_specs=placed, out_specs=P(("seq", "exp"), None), check_vma=False
    )
```

profile of v0, /device:TPU:0, one launch (start us, length us, event | category | flops | bytes accessed | tf_op | source)
XLA Modules:
  0.0 157.3 jit_solution(15832926701704818747)
XLA Ops:
  6.5 0.0 copy-start
  6.5 0.0 reduce-scatter.3.cloned.1.call-start
  6.5 0.8 convert_element_type.65
  7.4 0.8 copy.27
  8.1 0.2 reduce_window_sum.27
  8.3 0.6 slice.13
  8.9 1.2 dynamic-slice
  10.1 1.4 bitcast_dynamic-update-slice_fusion
  11.5 0.1 reduce.2
  11.6 11.4 %all-reduce = f32[4]{0:T(128)S(1)} all-reduce(f32[4]{0:T(128)S(1)} %bitcast_dynamic-update-slice_fusion), channel_id=1, replica_groups=mesh['seq'=4,'exp'=8] {'seq'}, use_global_device_ids=true, to_apply=%add | all-reduce | flops 4 | bytes 32 | tf_op jit(solution)/shard_map/reshape.20
  23.0 0.7 fusion.56
  23.7 1.1 convolution_convert_fusion.1
  24.8 7.5 %all-gather = bf16[512,128]{1,0:T(8,128)(2,1)S(1)} all-gather(bf16[128,128]{1,0:T(8,128)(2,1)S(1)} %convolution_convert_fusion.1), channel_id=2, replica_groups=mesh['seq'=4,'exp'=8] {'seq'}, dimensions={0}, use_global_device_ids=true | all-gather | bytes 163840 | tf_op jit(solution)/shard_map/all_gather | solution.py:39
  32.3 0.1 fusion.21
  32.4 0.4 fusion.27
  32.8 1.0 fusion.17
  33.8 1.1 multiply_reduce_fusion
  34.9 0.0 copy-start.2
  34.9 3.1 %fusion.38 = f32[128,4096]{1,0:T(8,128)} fusion(bf16[128,4096]{1,0:T(8,128)(2,1)} %param.16, f32[1,128,128]{2,1,0:T(8,128)S(1)} %get-tuple-element.12, f32[128]{0:T(128)S(1)} %convert_element_type.65, f32[128]{0:T(128)S(1)} %add_rsqrt_fusion), kind=kOutput, calls=%fused_computation.45 | convolution fusion | flops 134266880 | bytes 3212288 | tf_op jit(solution)/shard_map/dot_general | solution.py:65
  38.1 0.0 copy-start.3
  38.1 0.0 reduce-scatter.3.cloned.1.call-update
  38.1 0.0 all-gather.3.cloned.1.call-start
  38.1 36.2 %reduce-scatter.3.cloned.1.call-done = f32[16,4096]{1,0:T(8,128)} async-done(((f32[128,4096]{1,0:T(8,128)}), f32[16,4096]{1,0:T(8,128)}) %reduce-scatter.3.cloned.1.call-update) | async-done | bytes 262160 | tf_op jit(solution)/shard_map/reduce_scatter | solution.py:64
  74.3 1.6 %convert_element_type.67 = bf16[16,4096]{1,0:T(8,128)(2,1)} convert(f32[16,4096]{1,0:T(8,128)} %reduce-scatter.3.cloned.1.call-done) | non-fusion elementwise | flops 65536 | bytes 393216 | tf_op jit(solution)/shard_map/convert_element_type | solution.py:69
  75.9 0.0 all-gather.3.cloned.1.call-update
  76.0 0.0 reduce-scatter.5.cloned.1.call-start
  76.0 20.7 %all-gather.3.cloned.1.call-done = bf16[128,4096]{1,0:T(8,128)(2,1)} async-done(((bf16[16,4096]{1,0:T(8,128)(2,1)}), bf16[128,4096]{1,0:T(8,128)(2,1)}) %all-gather.3.cloned.1.call-update) | async-done | bytes 1048592 | tf_op jit(solution)/shard_map/all_gather | solution.py:70
  96.8 0.0 copy-done.2
  96.8 1.6 %fusion.57 = f32[128,4]{0,1:T(4,128)S(1)} fusion(bf16[128,4096]{1,0:T(8,128)(2,1)} %all-gather.3.cloned.1.call-done, bf16[4096,4]{0,1:T(4,128)(2,1)S(1)} %copy-done.2), kind=kOutput, calls=%fused_computation.75 | convolution fusion | flops 4194304 | bytes 1083392 | tf_op jit(solution)/shard_map/dot_general | solution.py:71
  98.4 0.0 copy-done.3
  98.5 0.1 copy.28
  98.6 0.1 reshape.164
  98.7 0.3 reduce-window.9
  99.0 0.1 slice.11
  99.1 0.1 reshape.161
  99.3 0.1 slice_reduce_fusion
  99.4 0.1 broadcast.80
  99.5 0.1 reshape.163
  99.6 0.1 copy.29
  99.7 1.6 %convolution_convert_fusion = bf16[96,4096]{1,0:T(8,128)(2,1)S(1)} fusion(bf16[128,4096]{1,0:T(8,128)(2,1)} %all-gather.3.cloned.1.call-done, f32[128,96]{0,1:T(8,128)S(1)} %convert_reduce_fusion), kind=kOutput, calls=%fused_computation.1 | convolution fusion | flops 101068800 | bytes 1884160 | tf_op jit(solution)/shard_map/dot_general | solution.py:84
  101.3 2.6 %fusion.4 = f32[96,288]{1,0:T(8,128)S(1)} fusion(bf16[96,4096]{1,0:T(8,128)(2,1)S(1)} %convolution_convert_fusion, bf16[1,4096,288]{1,2,0:T(8,128)(2,1)} %param.19), kind=kOutput, calls=%fused_computation.6 | convolution fusion | flops 226492416 | bytes 3256320 | tf_op jit(solution)/shard_map/dot_general | solution.py:87
  103.9 0.0 copy-done
  103.9 5.0 %fusion = f32[96,4096]{1,0:T(8,128)} fusion(bf16[1,288,4096]{2,1,0:T(8,128)(2,1)S(1)} %copy-done, bf16[96,4096]{1,0:T(8,128)(2,1)S(1)} %convolution_convert_fusion, bf16[1,4096,288]{1,2,0:T(8,128)(2,1)} %param.20, f32[96,288]{1,0:T(8,128)S(1)} %fusion.4), kind=kOutput, calls=%fused_computation.2 | convolution fusion | flops 453150720 | bytes 7188480 | tf_op jit(solution)/shard_map/dot_general | solution.py:90
  108.9 4.6 %convolution_multiply_fusion = f32[128,4096]{1,0:T(8,128)} fusion(f32[128,96]{0,1:T(8,128)S(1)} %convert_reduce_fusion, f32[96,4096]{1,0:T(8,128)} %fusion, f32[128]{0:T(128)S(1)} %get-tuple-element.5), kind=kOutput, calls=%fused_computation | convolution fusion | flops 604504064 | bytes 3719680 | tf_op jit(solution)/shard_map/dot_general | solution.py:91
  113.6 0.0 reduce-scatter.5.cloned.1.call-update
  113.6 35.6 %reduce-scatter.5.cloned.1.call-done = f32[16,4096]{1,0:T(8,128)} async-done(((f32[128,4096]{1,0:T(8,128)}), f32[16,4096]{1,0:T(8,128)}) %reduce-scatter.5.cloned.1.call-update) | async-done | bytes 262160 | tf_op jit(solution)/shard_map/reduce_scatter | solution.py:92
  149.2 0.0 copy-done.1
  149.2 1.6 %add_convert_fusion = bf16[16,4096]{1,0:T(8,128)(2,1)} fusion(f32[16,4096]{1,0:T(8,128)} %reduce-scatter.5.cloned.1.call-done, f32[16,4096]{1,0:T(8,128)S(1)} %copy-done.1), kind=kLoop, calls=%fused_computation.23 | loop fusion | flops 262144 | bytes 655360 | tf_op jit(solution)/shard_map/convert_element_type | solution.py:95
  (11 shorter events, 0.2 us)
Async XLA Ops:
  6.5 97.4 %copy-start = (bf16[1,288,4096]{2,1,0:T(8,128)(2,1)S(1)}, bf16[1,288,4096]{2,1,0:T(8,128)(2,1)}, u32[]{:S(2)}) copy-start(bf16[1,288,4096]{2,1,0:T(8,128)(2,1)} %param.21) | copy-start | bytes 7077892
  6.5 67.8 %reduce-scatter.3.cloned.1.call-start = ((), (), s32[]{:S(2)}) async-start(), calls=%async_computation.2 | async-start | bytes 2359296 | tf_op jit(solution)/shard_map/reduce_scatter | solution.py:64
  34.9 61.8 %copy-start.2 = (bf16[4096,4]{0,1:T(4,128)(2,1)S(1)}, bf16[4096,4]{0,1:T(4,128)(2,1)}, u32[]{:S(2)}) copy-start(bf16[4096,4]{0,1:T(4,128)(2,1)} %param.17) | copy-start | bytes 98308
  38.1 60.3 %copy-start.3 = (s32[128,2]{0,1:T(2,128)S(1)}, s32[128,2]{0,1:T(2,128)}, u32[]{:S(2)}) copy-start(s32[128,2]{0,1:T(2,128)} %param.18) | copy-start | bytes 3076
  38.1 58.7 %all-gather.3.cloned.1.call-start = ((), (), s32[]{:S(2)}) async-start(), calls=%async_computation.3 | async-start | bytes 1179648 | tf_op jit(solution)/shard_map/all_gather | solution.py:70
  76.0 73.2 %reduce-scatter.5.cloned.1.call-start = ((), (), s32[]{:S(2)}) async-start(), calls=%async_computation.4 | async-start | bytes 2359296 | tf_op jit(solution)/shard_map/reduce_scatter | solution.py:92
  108.9 40.2 %copy-start.1 = (f32[16,4096]{1,0:T(8,128)S(1)}, f32[16,4096]{1,0:T(8,128)}, u32[]{:S(2)}) copy-start(f32[16,4096]{1,0:T(8,128)} %reduce-scatter.3.cloned.1.call-done) | copy-start | bytes 786436
Sparse Core Ops, SparseCore 0:
  38.2 36.0 reduce-scatter.2
  76.1 20.6 all-gather.2
  113.7 35.3 reduce-scatter.4
where the time goes:
time: 158 us; the launch traced here: 157 us
  waiting for transfers between devices  92.5 us (59%)
  matrix products  22.3 us (14%)
  blocking collectives  18.9 us (12%)
  between operations  13.2 us (8%)
  other arithmetic  5.52 us (3%)
  local copies, waits for them, and re-layouts  4.77 us (3%)
    reduce_scatter x1, waiting for transfers between devices, local(): lax.psum_scatter(jnp.dot(normed, w_out, preferred_element_type=jnp.float3...  36.2 us
    reduce_scatter x1, waiting for transfers between devices, local(): lax.psum_scatter(token_gate[:, None] * spread_out, 'exp', scatter_dimensi...  35.6 us
    all_gather x1, waiting for transfers between devices, local(): mixed = lax.all_gather(own_mixed, 'exp', axis=0, tiled=True)  20.7 us
    another operation x1, blocking collectives  11.4 us
    all_gather x1, blocking collectives, local(): lax.all_gather(state_delta[None].astype(jnp.bfloat16), 'seq', axis=0, til...  7.52 us
    dot_general x1, matrix products, local(): slice_out = jnp.dot(hidden, w_down[0], preferred_element_type=jnp.float32)  5.03 us
    dot_general x1, matrix products, local(): jnp.dot(token_select, slice_out, precision=lax.Precision.HIGHEST)  4.65 us
    unnamed x12, local copies, waits for them, and re-layouts  3.38 us
  transfers between devices with their start and end apart: 3, of which 3 were waited for; matrix products, arithmetic and copies ran while one was open for 0% of the time, Pallas kernels for 0%

commit v1 on v0

--- a/solution.py
+++ b/solution.py
@@ -1,10 +1,20 @@
+import functools
+
 import jax
 import jax.numpy as jnp
 from jax import lax
+from jax.experimental import pallas as pl
+from jax.experimental.pallas import tpu as pltpu
 from jax.sharding import PartitionSpec as P
 
-
-def local(query, key_in, value, decay_log, norm_gain, w_out, router, routes, w_gate, w_up, w_down):
+F32 = jnp.float32
+BF16 = jnp.bfloat16
+TILE_ROWS = 16
+COLUMNS = 1024
+VMEM_LIMIT = 16 * 1024 * 1024
+
+
+def plain_plan(query, key_in, value, decay_log, norm_gain, w_out, router, routes, w_gate, w_up, w_down):
     tok_count = query.shape[0]
     head_count = decay_log.shape[1]
     head_size = query.shape[1] // head_count
@@ -95,6 +105,365 @@
     return (own_mixed.astype(jnp.float32) + summed).astype(jnp.bfloat16)
 
 
+def iota2(shape, axis):
+    return lax.broadcasted_iota(jnp.int32, shape, axis)
+
+
+def cumulate(decay_row):
+    t = decay_row.shape[1]
+    row, col = iota2((t, t), 0), iota2((t, t), 1)
+    spread = jnp.broadcast_to(decay_row, (t, t))
+    column = jnp.sum(jnp.where(col <= row, spread, 0.0), axis=1, keepdims=True)
+    own = jnp.sum(jnp.where(col == row, spread, 0.0), axis=1, keepdims=True)
+    line = jnp.sum(jnp.where(row <= col, own, 0.0), axis=0, keepdims=True)
+    return column, line
+
+
+def dot_f32(a, b, dims):
+    return lax.dot_general(a, b, (dims, ((), ())), preferred_element_type=F32)
+
+
+def split_dot(a_f32, b, dims):
+    high = a_f32.astype(BF16)
+    low = (a_f32 - high.astype(F32)).astype(BF16)
+    return dot_f32(high, b, dims) + dot_f32(low, b, dims)
+
+
+def dma_in(sems, pairs):
+    copies = [pltpu.make_async_copy(a, b, sems.at[i]) for i, (a, b) in enumerate(pairs)]
+    for copy in copies:
+        copy.start()
+    return copies
+
+
+def put_state(out_ref, state, total):
+    d = state.shape[1]
+    out_ref[0:d, :] = state.astype(BF16)
+    wide = jnp.broadcast_to(total, (TILE_ROWS, d))
+    part0 = wide.astype(BF16).astype(F32)
+    part1 = (wide - part0).astype(BF16).astype(F32)
+    part2 = wide - part0 - part1
+    row = iota2((TILE_ROWS, d), 0)
+    parts = jnp.where(row == 0, part0, jnp.where(row == 1, part1, jnp.where(row == 2, part2, 0.0)))
+    out_ref[d:, :] = parts.astype(BF16)
+
+
+def get_state(ref):
+    d = ref.shape[1]
+    return ref[0:d, :].astype(F32), jnp.sum(ref[d:, :].astype(F32), axis=0, keepdims=True)
+
+
+def state_kernel(key_hbm, value_hbm, decay_hbm, out_ref, key_ref, value_ref, decay_ref, sems):
+    t, d = key_ref.shape
+    copies = dma_in(sems, [(decay_hbm, decay_ref), (key_hbm, key_ref), (value_hbm, value_ref)])
+    for copy in copies:
+        copy.wait()
+    column, _ = cumulate(decay_ref[...])
+    total = column[t - 1 :, :]
+    keyed = key_ref[...].astype(F32) * jnp.exp(total - column)
+    put_state(out_ref, split_dot(keyed, value_ref[...], ((0,), (0,))), jnp.broadcast_to(total, (1, d)))
+
+
+def take_before(bit, other_ref, before):
+    state, total = get_state(other_ref)
+    incoming, log = before
+    earlier = jnp.bitwise_and(lax.axis_index("seq"), bit) > 0
+    grown = jnp.where(earlier, jnp.exp(log) * state, 0.0)
+    more = jnp.where(earlier, total, 0.0)
+    if incoming is None:
+        return grown, more
+    return incoming + grown, log + more
+
+
+def merge_kernel(bit, mine_ref, other_ref, *refs):
+    out_ref, incoming_ref, log_ref = refs[-3:]
+    d = incoming_ref.shape[1]
+    before = (None, jnp.zeros((1, d), F32)) if len(refs) == 3 else (refs[0][...], refs[1][0:1, :])
+    incoming, log = take_before(bit, other_ref, before)
+    incoming_ref[...] = incoming
+    log_ref[...] = jnp.broadcast_to(log, log_ref.shape)
+    mine, my_total = get_state(mine_ref)
+    other, other_total = get_state(other_ref)
+    earlier = jnp.bitwise_and(lax.axis_index("seq"), bit) > 0
+    later_total = jnp.where(earlier, my_total, other_total)
+    merged = jnp.exp(later_total) * jnp.where(earlier, other, mine) + jnp.where(earlier, mine, other)
+    put_state(out_ref, merged, my_total + other_total)
+
+
+def within_kernel(
+    query_hbm, key_hbm, value_hbm, decay_hbm, gain_hbm, w_out_hbm, _,
+    intra_ref, grown_ref, query_ref, gain_ref, w_out_ref,
+    key_ref, value_ref, decay_ref, gain_in_ref, sems,
+):
+    t, d = query_ref.shape
+    copies = dma_in(
+        sems,
+        [
+            (decay_hbm, decay_ref),
+            (query_hbm, query_ref),
+            (key_hbm, key_ref),
+            (value_hbm, value_ref),
+            (gain_hbm, gain_in_ref),
+            (w_out_hbm, w_out_ref),
+        ],
+    )
+    for copy in copies[:5]:
+        copy.wait()
+    column, line = cumulate(decay_ref[...])
+    query, key, value = query_ref[...], key_ref[...], value_ref[...]
+    scores = dot_f32(query, key, ((1,), (1,)))
+    causal = iota2((t, t), 0) >= iota2((t, t), 1)
+    weights = jnp.where(causal, jnp.exp(jnp.where(causal, column - line, 0.0)), 0.0)
+    attend = (scores * weights * (1.0 / d)).astype(BF16)
+    intra_ref[...] = dot_f32(attend, value, ((1,), (0,)))
+    grown_ref[...] = jnp.broadcast_to(jnp.exp(column) * (1.0 / d), (t, d))
+    gain_ref[...] = jnp.broadcast_to(gain_in_ref[...].astype(F32), gain_ref.shape)
+    copies[5].wait()
+
+
+def places(step, core, n_pair):
+    bits = n_pair.bit_length() - 1
+    flipped = sum(((step >> i) & 1) << (bits - 1 - i) for i in range(bits))
+    return step + core * (flipped - step)
+
+
+def place_matrix(rows, n_pair, pair, core):
+    size = 2 * n_pair * rows
+    i, j = iota2((size, size), 0), iota2((size, size), 1)
+    half, inner = i // (n_pair * rows), i % (n_pair * rows)
+    whose = (core + half) % 2
+    who = jnp.bitwise_xor(places(inner // rows, whose, n_pair), pair)
+    source = (2 * who + whose) * rows + inner % rows
+    return jnp.where(source == j, 1.0, 0.0).astype(BF16)
+
+
+def fetch_kernel(
+    n_pair, slices, router_hbm, routes_hbm, gate_hbm, up_hbm, down_hbm, _,
+    in_ref, down_ref, member_ref, router_ref, routes_ref, sems,
+):
+    hid = gate_hbm.shape[0]
+    copies = dma_in(
+        sems,
+        [
+            (router_hbm, router_ref),
+            (routes_hbm, routes_ref),
+            (gate_hbm, in_ref.at[0:hid]),
+            (up_hbm, in_ref.at[hid : 2 * hid]),
+            (down_hbm, down_ref),
+        ],
+    )
+    for copy in copies[:2]:
+        copy.wait()
+    experts, t = router_ref.shape[0], routes_ref.shape[1]
+    in_ref[2 * hid :, :] = jnp.zeros((TILE_ROWS, in_ref.shape[1]), BF16)
+    in_ref[2 * hid : 2 * hid + experts, :] = router_ref[...]
+    padded = member_ref.shape[0]
+    hits = jnp.zeros((padded, t), F32)
+    for k in range(routes_ref.shape[0]):
+        hits = hits + jnp.where(routes_ref[k : k + 1, :] == iota2((padded, t), 0), 1.0, 0.0)
+    exp_index = lax.axis_index("exp")
+    place = place_matrix(t // (2 * n_pair), n_pair, exp_index // 2, exp_index % 2)
+    member_ref[...] = dot_f32(hits.astype(BF16), place, ((1,), (1,)))
+    for copy in copies[2:]:
+        copy.wait()
+
+
+def project_kernel(
+    n_pair, bit, other_ref, incoming_ref, log_ref, intra_ref, grown_ref, query_ref, gain_ref, w_ref, mine_ref, theirs_ref
+):
+    t, d = query_ref.shape
+    incoming, _ = take_before(bit, other_ref, (incoming_ref[...], log_ref[0:1, :]))
+    high = incoming.astype(BF16)
+    low = (incoming - high.astype(F32)).astype(BF16)
+    query = query_ref[...]
+    read = dot_f32(query, high, ((1,), (0,))) + dot_f32(query, low, ((1,), (0,)))
+    attended = intra_ref[...] + grown_ref[...] * read
+    inverse = lax.rsqrt(jnp.mean(attended * attended, axis=1, keepdims=True) + 1e-06)
+    normed = (attended * inverse * gain_ref[0:1, :]).astype(BF16)
+    exp_index = lax.axis_index("exp")
+    place = place_matrix(t // (2 * n_pair), n_pair, exp_index // 2, exp_index % 2)
+    normed = dot_f32(place, normed, ((1,), (0,))).astype(BF16)
+    for at in chunks(w_ref.shape[1]):
+        part = dot_f32(normed, w_ref[:, at], ((1,), (0,))).astype(BF16)
+        mine_ref[:, at] = part[: t // 2]
+        theirs_ref[:, at] = part[t // 2 :]
+
+
+def chunks(width):
+    size = min(width, COLUMNS)
+    return [slice(i, i + size) for i in range(0, width, size)]
+
+
+def add_kernel(groups, a_ref, b_ref, *refs):
+    outs = refs[-len(groups) :]
+    rows = outs[0].shape[0] // len(groups[0])
+    for group, ref in zip(groups, outs):
+        for i, block in enumerate(group):
+            at = slice(block * rows, (block + 1) * rows)
+            total = a_ref[at, :].astype(F32) + b_ref[at, :].astype(F32)
+            ref[i * rows : (i + 1) * rows, :] = total.astype(ref.dtype)
+
+
+def join_kernel(*refs):
+    start = 0
+    for ref in refs[:-1]:
+        refs[-1][start : start + ref.shape[0], :] = ref[...]
+        start += ref.shape[0]
+
+
+def expert_kernel(slices, experts, order, rows, in_ref, down_ref, member_ref, *refs):
+    parts, (mine_ref, theirs_ref) = refs[:-2], refs[-2:]
+    half = len(parts) // 2
+    hid, width = down_ref.shape
+    t = member_ref.shape[1]
+    total = jnp.zeros((in_ref.shape[0], t), F32)
+    for at in chunks(width):
+        blocks = [
+            parts[core * half + part][i * rows : (i + 1) * rows, at] for core in range(2) for part, i in order
+        ]
+        total = total + dot_f32(in_ref[:, at], jnp.concatenate(blocks, axis=0), ((1,), (1,)))
+    gate, up, logits = total[0:hid], total[hid : 2 * hid], total[2 * hid : 2 * hid + experts]
+    raised = jnp.where(member_ref[0:experts, :] > 0.5, jnp.exp(logits), 0.0)
+    mine = iota2((experts, t), 0) == lax.axis_index("exp") // slices
+    prob = jnp.sum(jnp.where(mine, raised, 0.0), axis=0, keepdims=True) / jnp.sum(raised, axis=0, keepdims=True)
+    hidden = (gate / (1.0 + jnp.exp(-gate)) * up * prob).astype(BF16)
+    for at in chunks(width):
+        part = dot_f32(hidden, down_ref[:, at], ((0,), (0,))).astype(BF16)
+        mine_ref[:, at] = part[: t // 2]
+        theirs_ref[:, at] = part[t // 2 :]
+
+
+def result_kernel(kept_ref, moved_ref, mixed_ref, out_ref):
+    total = kept_ref[...].astype(F32) + moved_ref[...].astype(F32) + mixed_ref[...].astype(F32)
+    out_ref[...] = total.astype(BF16)
+
+
+def call(kernel, outs, args, scratch=(), flops=0, far=0):
+    whole = pl.BlockSpec(memory_space=pltpu.VMEM)
+    size = sum(a.size * a.dtype.itemsize for a in (*args, *outs))
+    if far:
+        args = [pltpu.with_memory_space_constraint(a, pltpu.HBM) for a in args[:far]] + list(args[far:])
+    return pl.pallas_call(
+        kernel,
+        out_shape=outs,
+        in_specs=[pl.BlockSpec(memory_space=pl.ANY) if far else whole] * len(args),
+        out_specs=[whole] * len(outs),
+        scratch_shapes=list(scratch),
+        compiler_params=pltpu.CompilerParams(vmem_limit_bytes=VMEM_LIMIT),
+        cost_estimate=pl.CostEstimate(flops=flops, bytes_accessed=size, transcendentals=0),
+    )(*args)
+
+
+def local(query, key_in, value, decay_log, norm_gain, w_out, router, routes, w_gate, w_up, w_down):
+    t, d = query.shape
+    width = w_out.shape[1]
+    exp_count, seq_count = lax.axis_size("exp"), lax.axis_size("seq")
+    n_pair = exp_count // 2
+    rows = t // exp_count
+    experts = router.shape[1]
+    slices = exp_count // experts
+    hid = w_gate.shape[2]
+    out = jax.ShapeDtypeStruct
+    dma = pltpu.SemaphoreType.DMA
+    bits = [1 << i for i in range(n_pair.bit_length() - 1)]
+
+    def swap(x, bit):
+        flips = (2 * bit, 2 * places(bit, 1, n_pair))
+        return lax.ppermute(x, "exp", [(e, e ^ flips[e % 2]) for e in range(exp_count)])
+
+    def across(x):
+        return lax.ppermute(x, "exp", [(e, e ^ 1) for e in range(exp_count)])
+
+    def add(a, b, groups, after=()):
+        outs = [out((len(group) * rows, width), BF16) for group in groups]
+        return call(functools.partial(add_kernel, groups), outs, (a, b, *after))
+
+    def deal(held, bit):
+        return [[i for i, r in enumerate(held) if bool(r & bit) == gone] for gone in (False, True)]
+
+    decay_row = decay_log.T
+    block = pltpu.VMEM((t, d), BF16)
+    decay_block = pltpu.VMEM((1, t), F32)
+    group = out((d + TILE_ROWS, d), BF16)
+    (state,) = call(
+        state_kernel, [group], (key_in, value, decay_row), [block, block, decay_block, dma((3,))], far=3
+    )
+
+    def from_rank(x, bit):
+        return lax.ppermute(x, "seq", [(i, i ^ bit) for i in range(seq_count)])
+
+    seq_bits = [1 << i for i in range(seq_count.bit_length() - 1)]
+    other = from_rank(state, seq_bits[0])
+    intra, grown, query_near, gain, w_out_near = call(
+        within_kernel,
+        [out((t, d), F32), out((t, d), F32), out((t, d), BF16), out((8, d), F32), out(w_out.shape, BF16)],
+        (query, key_in, value, decay_row, norm_gain[None, :], w_out, state),
+        [block, block, decay_block, pltpu.VMEM((1, d), BF16), dma((6,))],
+        far=6,
+    )
+    before = ()
+    for bit, later in zip(seq_bits, seq_bits[1:]):
+        state, *before = call(
+            functools.partial(merge_kernel, bit), [group, out((d, d), F32), out((8, d), F32)], (state, other, *before)
+        )
+        other = from_rank(state, later)
+    half = out((t // 2, width), BF16)
+    mine, theirs = call(
+        functools.partial(project_kernel, n_pair, seq_bits[-1]),
+        [half, half],
+        (other, *before, intra, grown, query_near, gain, w_out_near),
+        flops=2 * t * d * width,
+    )
+
+    def reduce(mine, theirs, after):
+        held = list(range(n_pair))
+        kept, moved = mine, across(theirs)
+        extra = ()
+        for step, bit in enumerate(bits):
+            groups = deal(held, bit)
+            kept, go = add(kept, moved, groups, extra)
+            held = [held[i] for i in groups[0]]
+            moved = swap(go, bit)
+            if step == 0:
+                extra = after(go)
+        return kept, moved
+
+    near = []
+
+    def fetch(go):
+        near.extend(
+            call(
+                functools.partial(fetch_kernel, n_pair, slices),
+                [out((2 * hid + TILE_ROWS, width), BF16), out((hid, width), BF16), out((-(-experts // 8) * 8, t), F32)],
+                (router.T, routes.T, w_gate[0].T, w_up[0].T, w_down[0], go),
+                [pltpu.VMEM((experts, width), BF16), pltpu.VMEM((routes.shape[1], t), jnp.int32), dma((5,))],
+                far=5,
+            )
+        )
+        return (near[2],)
+
+    (mixed,) = add(*reduce(mine, theirs, fetch), [[0]])
+
+    held = [0]
+    whole = mixed
+    for step, bit in enumerate(reversed(bits)):
+        moved = swap(whole, bit)
+        held = held + [r ^ bit for r in held]
+        if step + 1 < len(bits):
+            (whole,) = call(join_kernel, [out((2 * whole.shape[0], width), BF16)], (whole, moved))
+    parts = [whole, moved]
+    spots = [(n, i) for n, part in enumerate(parts) for i in range(part.shape[0] // rows)]
+    order = [spots[held.index(r)] for r in range(n_pair)]
+    mine, theirs = call(
+        functools.partial(expert_kernel, slices, experts, order, rows),
+        [half, half],
+        (*near, *parts, *[across(part) for part in parts]),
+        flops=6 * t * hid * width,
+    )
+    kept, moved = reduce(mine, theirs, lambda go: ())
+    return call(result_kernel, [out((rows, width), BF16)], (kept, moved, mixed))[0]
+
+
 def solution(mesh):
     placed = (
         P("seq", "exp"),
@@ -109,6 +478,16 @@
         P("exp", None, None),
         P("exp", None, None),
     )
+
+    def pick(query, key_in, value, decay_log, *rest):
+        rows = query.shape[0] // lax.axis_size("exp")
+        exp_count = lax.axis_size("exp")
+        tiled = rows % TILE_ROWS == 0 and decay_log.shape[1] == 1
+        for count in (exp_count, lax.axis_size("seq")):
+            tiled = tiled and count >= 4 and count & (count - 1) == 0
+        plan = local if tiled else plain_plan
+        return plan(query, key_in, value, decay_log, *rest)
+
     return jax.shard_map(
-        local, mesh=mesh, in_specs=placed, out_specs=P(("seq", "exp"), None), check_vma=False
-    )
+        pick, mesh=mesh, in_specs=placed, out_specs=P(("seq", "exp"), None), check_vma=False
+    )

time: 158 us -> 69 us (0.44)
  the two profiles are of different devices: /device:TPU:0 before, /device:TPU:2 now
where the time goes in v1:
time: 69 us; the launch traced here: 68.8 us
  waiting for transfers between devices  49.5 us (72%)
  Pallas kernels  10.8 us (16%)
  starting transfers between devices  8.34 us (12%)
    ppermute x6, waiting for transfers between devices, swap(): lax.ppermute(x, 'exp', [(e, e ^ flips[e % 2]) for e in range(exp_count)])  39.3 us
    pallas_call x13, Pallas kernels, call(): pl.pallas_call(kernel, out_shape=outs, in_specs=[pl.BlockSpec(memory_spac...  10.8 us
    ppermute x6, starting transfers between devices, swap(): lax.ppermute(x, 'exp', [(e, e ^ flips[e % 2]) for e in range(exp_count)])  6.38 us
    ppermute x4, waiting for transfers between devices, across(): return lax.ppermute(x, 'exp', [(e, e ^ 1) for e in range(exp_count)])  5.2 us
    ppermute x2, waiting for transfers between devices, from_rank(): return lax.ppermute(x, 'seq', [(i, i ^ bit) for i in range(seq_count)])  5.01 us
    ppermute x2, starting transfers between devices, from_rank(): return lax.ppermute(x, 'seq', [(i, i ^ bit) for i in range(seq_count)])  1.65 us
  transfers between devices with their start and end apart: 12, of which 11 were waited for; matrix products, arithmetic and copies ran while one was open for 0% of the time, Pallas kernels for 7%

profile of v1, /device:TPU:2, one launch (start us, length us, event | category | flops | bytes accessed | tf_op | source)
XLA Modules:
  0.0 68.8 jit_solution(4227670168707065011)
XLA Ops:
  0.0 1.1 %shard_map.109.mine_ref._ = bf16[144,128]{1,0:T(8,128)(2,1)S(1)} custom-call(bf16[128,128]{1,0:T(8,128)(2,1)} %key_hbm.3, bf16[128,128]{1,0:T(8,128)(2,1)} %value_hbm.3, f32[1,128]{1,0:T(1,128)} %bitcast.15), custom_call_target="tpu_custom_call" | custom-call | bytes 102912 | tf_op jit(solution)/shard_map/pallas_call | solution.py:346
  1.1 0.1 collective-permute-start
  1.2 3.9 %collective-permute-done.other_ref = bf16[144,128]{1,0:T(8,128)(2,1)S(1)} collective-permute-done((bf16[144,128]{1,0:T(8,128)(2,1)S(1)}, bf16[144,128]{1,0:T(8,128)(2,1)S(1)}, u32[]{:S(2)}, u32[]{:S(2)}) %collective-permute-start) | collective-permute-done | bytes 36896 | tf_op jit(solution)/shard_map/ppermute | solution.py:393
  5.2 1.6 %collective-permute-start.1 = (bf16[144,128]{1,0:T(8,128)(2,1)S(1)}, bf16[144,128]{1,0:T(8,128)(2,1)S(1)}, u32[]{:S(2)}, u32[]{:S(2)}) collective-permute-start(bf16[144,128]{1,0:T(8,128)(2,1)S(1)} %get-tuple-element.28), channel_id=1, source_target_pairs={{0,16},{8,24},{16,0},{24,8},{1,17},{9,25},{17,1},{25,9},{2,18},{10... | collective-permute-start | bytes 110600 | tf_op jit(solution)/shard_map/ppermute | solution.py:393
  6.8 1.4 %shard_map.111 = (f32[128,128]{1,0:T(8,128)S(1)}, f32[128,128]{1,0:T(8,128)S(1)}, bf16[128,128]{1,0:T(8,128)(2,1)S(1)}, f32[8,128]{1,0:T(8,128)S(1)}, bf16[128,4096]{1,0:T(8,128)(2,1)S(1)}) custom-call(bf16[128,128]{1,0:T(8,128)(2,1)} %query_hbm.1, bf16[128,128]{1,0:T(8,128)(2,1)} %key_hbm.3, bf16[128,128]{1,0:T(8,128)(2,1)} %value_hbm.3, ...), custom_call_target="tpu_custom_call" | custom-call | bytes 2401024 | tf_op jit(solution)/shard_map/pallas_call | solution.py:346
  8.1 1.1 %collective-permute-done.1.other_ref = bf16[144,128]{1,0:T(8,128)(2,1)S(1)} collective-permute-done((bf16[144,128]{1,0:T(8,128)(2,1)S(1)}, bf16[144,128]{1,0:T(8,128)(2,1)S(1)}, u32[]{:S(2)}, u32[]{:S(2)}) %collective-permute-start.1) | collective-permute-done | bytes 36896 | tf_op jit(solution)/shard_map/ppermute | solution.py:393
  9.2 0.8 %shard_map.112 = (bf16[64,4096]{1,0:T(8,128)(2,1)S(1)}, bf16[64,4096]{1,0:T(8,128)(2,1)S(1)}) custom-call(bf16[144,128]{1,0:T(8,128)(2,1)S(1)} %collective-permute-done.1.other_ref, f32[128,128]{1,0:T(8,128)S(1)} %get-tuple-element.29.incoming_ref, f32[8,128]{1,0:T(8,128)S(1)} %get-tuple-element.30.log_ref, f32[128,128]{1,0:T(8,128)S(1)} %get-tuple-element.31.intra_ref, ...), custom_call_target="tpu_custom_call" | custom-call | flops 134217728 | bytes 2371584 | tf_op jit(solution)/shard_map/pallas_call | solution.py:346
  10.0 0.1 collective-permute-start.2
  10.1 1.9 %collective-permute-done.2.b_ref = bf16[64,4096]{1,0:T(8,128)(2,1)S(1)} collective-permute-done((bf16[64,4096]{1,0:T(8,128)(2,1)S(1)}, bf16[64,4096]{1,0:T(8,128)(2,1)S(1)}, u32[]{:S(2)}, u32[]{:S(2)}) %collective-permute-start.2) | collective-permute-done | bytes 524320 | tf_op jit(solution)/shard_map/ppermute | solution.py:375
  12.0 0.1 shard_map.113
  12.1 1.6 %collective-permute-start.3 = (bf16[32,4096]{1,0:T(8,128)(2,1)S(1)}, bf16[32,4096]{1,0:T(8,128)(2,1)S(1)}, u32[]{:S(2)}, u32[]{:S(2)}) collective-permute-start(bf16[32,4096]{1,0:T(8,128)(2,1)S(1)} %get-tuple-element.38._), channel_id=1, source_target_pairs={{0,2},{1,5},{2,0},{3,7},{4,6},{5,1},{6,4},{7,3},{8,10},{9,13},{10,... | collective-permute-start | bytes 786440 | tf_op jit(solution)/shard_map/ppermute | solution.py:372
  13.8 3.2 %shard_map.114 = (bf16[592,4096]{1,0:T(8,128)(2,1)S(1)}, bf16[288,4096]{1,0:T(8,128)(2,1)S(1)}, f32[8,128]{1,0:T(8,128)S(1)}) custom-call(bf16[4,4096]{1,0:T(4,128)(2,1)} %bitcast.14, s32[2,128]{1,0:T(2,128)} %bitcast.17, bf16[288,4096]{1,0:T(8,128)(2,1)} %bitcast.11, bf16[288,4096]{1,0:T(8,128)(2,1)} %bitcast.12, bf16[288,4096]{1,0:T(8,128)(2,1)} %bitcast.13, ...), custom_call_target="tpu_custom_call" | custom-call | bytes 14586880 | tf_op jit(solution)/shard_map/pallas_call | solution.py:346
  16.9 4.4 %collective-permute-done.3.b_ref = bf16[32,4096]{1,0:T(8,128)(2,1)S(1)} collective-permute-done((bf16[32,4096]{1,0:T(8,128)(2,1)S(1)}, bf16[32,4096]{1,0:T(8,128)(2,1)S(1)}, u32[]{:S(2)}, u32[]{:S(2)}) %collective-permute-start.3) | collective-permute-done | bytes 262176 | tf_op jit(solution)/shard_map/ppermute | solution.py:372
  21.3 0.1 shard_map.115
  21.4 1.8 %collective-permute-start.4 = (bf16[16,4096]{1,0:T(8,128)(2,1)S(1)}, bf16[16,4096]{1,0:T(8,128)(2,1)S(1)}, u32[]{:S(2)}, u32[]{:S(2)}) collective-permute-start(bf16[16,4096]{1,0:T(8,128)(2,1)S(1)} %get-tuple-element.44), channel_id=1, source_target_pairs={{0,4},{1,3},{2,6},{3,1},{4,0},{5,7},{6,2},{7,5},{8,12},{9,11},{10,... | collective-permute-start | bytes 393224 | tf_op jit(solution)/shard_map/ppermute | solution.py:372
  23.2 4.7 %collective-permute-done.4.b_ref = bf16[16,4096]{1,0:T(8,128)(2,1)S(1)} collective-permute-done((bf16[16,4096]{1,0:T(8,128)(2,1)S(1)}, bf16[16,4096]{1,0:T(8,128)(2,1)S(1)}, u32[]{:S(2)}, u32[]{:S(2)}) %collective-permute-start.4) | collective-permute-done | bytes 131104 | tf_op jit(solution)/shard_map/ppermute | solution.py:372
  27.9 1.3 %collective-permute-start.5 = (bf16[16,4096]{1,0:T(8,128)(2,1)S(1)}, bf16[16,4096]{1,0:T(8,128)(2,1)S(1)}, u32[]{:S(2)}, u32[]{:S(2)}) collective-permute-start(bf16[16,4096]{1,0:T(8,128)(2,1)S(1)} %shard_map.116.refs_0_.mixed_ref), channel_id=1, source_target_pairs={{0,4},{1,3},{2,6},{3,1},{4,0},{5,7},{6,2},{7,5},{8,12},{9,11},{10,... | collective-permute-start | bytes 393224 | tf_op jit(solution)/shard_map/ppermute | solution.py:372
  29.2 9.2 %collective-permute-done.5.refs_1_ = bf16[16,4096]{1,0:T(8,128)(2,1)S(1)} collective-permute-done((bf16[16,4096]{1,0:T(8,128)(2,1)S(1)}, bf16[16,4096]{1,0:T(8,128)(2,1)S(1)}, u32[]{:S(2)}, u32[]{:S(2)}) %collective-permute-start.5) | collective-permute-done | bytes 131104 | tf_op jit(solution)/shard_map/ppermute | solution.py:372
  38.4 0.1 collective-permute-start.6
  38.5 0.0 collective-permute-start.7
  38.6 6.3 %collective-permute-done.6.refs_1_ = bf16[32,4096]{1,0:T(8,128)(2,1)S(1)} collective-permute-done((bf16[32,4096]{1,0:T(8,128)(2,1)S(1)}, bf16[32,4096]{1,0:T(8,128)(2,1)S(1)}, u32[]{:S(2)}, u32[]{:S(2)}) %collective-permute-start.6) | collective-permute-done | bytes 262176 | tf_op jit(solution)/shard_map/ppermute | solution.py:372
  44.9 0.0 collective-permute-start.8
  44.9 0.0 collective-permute-done.7.refs_2_
  44.9 1.5 %collective-permute-done.8.refs_3_ = bf16[32,4096]{1,0:T(8,128)(2,1)S(1)} collective-permute-done((bf16[32,4096]{1,0:T(8,128)(2,1)S(1)}, bf16[32,4096]{1,0:T(8,128)(2,1)S(1)}, u32[]{:S(2)}, u32[]{:S(2)}) %collective-permute-start.8) | collective-permute-done | bytes 262176 | tf_op jit(solution)/shard_map/ppermute | solution.py:375
  46.4 3.2 %shard_map.118 = (bf16[64,4096]{1,0:T(8,128)(2,1)S(1)}, bf16[64,4096]{1,0:T(8,128)(2,1)S(1)}) custom-call(bf16[592,4096]{1,0:T(8,128)(2,1)S(1)} %get-tuple-element.39.in_ref, bf16[288,4096]{1,0:T(8,128)(2,1)S(1)} %get-tuple-element.40.down_ref, f32[8,128]{1,0:T(8,128)S(1)} %get-tuple-element.41.refs_0_.member_ref, bf16[32,4096]{1,0:T(8,128)(2,1)S(1)} %shard_map.117.refs_0_, ...), custom_call_target="tpu_custom_call" | custom-call | flops 905969664 | bytes 9310208 | tf_op jit(solution)/shard_map/pallas_call | solution.py:346
  49.6 0.2 collective-permute-start.9
  49.8 1.8 %collective-permute-done.9.b_ref = bf16[64,4096]{1,0:T(8,128)(2,1)S(1)} collective-permute-done((bf16[64,4096]{1,0:T(8,128)(2,1)S(1)}, bf16[64,4096]{1,0:T(8,128)(2,1)S(1)}, u32[]{:S(2)}, u32[]{:S(2)}) %collective-permute-start.9) | collective-permute-done | bytes 524320 | tf_op jit(solution)/shard_map/ppermute | solution.py:375
  51.6 0.1 shard_map.119
  51.7 0.1 collective-permute-start.10
  51.9 8.8 %collective-permute-done.10.b_ref = bf16[32,4096]{1,0:T(8,128)(2,1)S(1)} collective-permute-done((bf16[32,4096]{1,0:T(8,128)(2,1)S(1)}, bf16[32,4096]{1,0:T(8,128)(2,1)S(1)}, u32[]{:S(2)}, u32[]{:S(2)}) %collective-permute-start.10) | collective-permute-done | bytes 262176 | tf_op jit(solution)/shard_map/ppermute | solution.py:372
  60.7 0.1 shard_map.120
  60.7 1.4 %collective-permute-start.11 = (bf16[16,4096]{1,0:T(8,128)(2,1)S(1)}, bf16[16,4096]{1,0:T(8,128)(2,1)S(1)}, u32[]{:S(2)}, u32[]{:S(2)}) collective-permute-start(bf16[16,4096]{1,0:T(8,128)(2,1)S(1)} %get-tuple-element.50), channel_id=1, source_target_pairs={{0,4},{1,3},{2,6},{3,1},{4,0},{5,7},{6,2},{7,5},{8,12},{9,11},{10,... | collective-permute-start | bytes 393224 | tf_op jit(solution)/shard_map/ppermute | solution.py:372
  62.1 6.0 %collective-permute-done.11.moved_ref = bf16[16,4096]{1,0:T(8,128)(2,1)S(1)} collective-permute-done((bf16[16,4096]{1,0:T(8,128)(2,1)S(1)}, bf16[16,4096]{1,0:T(8,128)(2,1)S(1)}, u32[]{:S(2)}, u32[]{:S(2)}) %collective-permute-start.11) | collective-permute-done | bytes 131104 | tf_op jit(solution)/shard_map/ppermute | solution.py:372
  68.1 0.7 %shard_map.121 = bf16[16,4096]{1,0:T(8,128)(2,1)} custom-call(bf16[16,4096]{1,0:T(8,128)(2,1)S(1)} %get-tuple-element.49.kept_ref, bf16[16,4096]{1,0:T(8,128)(2,1)S(1)} %collective-permute-done.11.moved_ref, bf16[16,4096]{1,0:T(8,128)(2,1)S(1)} %shard_map.116.refs_0_.mixed_ref), custom_call_target="tpu_custom_call" | custom-call | bytes 524288 | tf_op jit(solution)/shard_map/pallas_call | solution.py:346
  (3 shorter events, 0.1 us)
Async XLA Ops:
  1.1 4.0 %collective-permute-start = (bf16[144,128]{1,0:T(8,128)(2,1)S(1)}, bf16[144,128]{1,0:T(8,128)(2,1)S(1)}, u32[]{:S(2)}, u32[]{:S(2)}) collective-permute-start(bf16[144,128]{1,0:T(8,128)(2,1)S(1)} %shard_map.109.mine_ref._), channel_id=1, source_target_pairs={{0,8},{8,0},{16,24},{24,16},{1,9},{9,1},{17,25},{25,17},{2,10},{10... | collective-permute-start | bytes 110600 | tf_op jit(solution)/shard_map/ppermute | solution.py:393
  5.2 4.0 %collective-permute-start.1 = (bf16[144,128]{1,0:T(8,128)(2,1)S(1)}, bf16[144,128]{1,0:T(8,128)(2,1)S(1)}, u32[]{:S(2)}, u32[]{:S(2)}) collective-permute-start(bf16[144,128]{1,0:T(8,128)(2,1)S(1)} %get-tuple-element.28), channel_id=1, source_target_pairs={{0,16},{8,24},{16,0},{24,8},{1,17},{9,25},{17,1},{25,9},{2,18},{10... | collective-permute-start | bytes 110600 | tf_op jit(solution)/shard_map/ppermute | solution.py:393
  10.0 2.0 %collective-permute-start.2 = (bf16[64,4096]{1,0:T(8,128)(2,1)S(1)}, bf16[64,4096]{1,0:T(8,128)(2,1)S(1)}, u32[]{:S(2)}, u32[]{:S(2)}) collective-permute-start(bf16[64,4096]{1,0:T(8,128)(2,1)S(1)} %get-tuple-element.37), channel_id=1, source_target_pairs={{0,1},{1,0},{2,3},{3,2},{4,5},{5,4},{6,7},{7,6},{8,9},{9,8},{10,11... | collective-permute-start | bytes 1572872 | tf_op jit(solution)/shard_map/ppermute | solution.py:375
  12.1 9.2 %collective-permute-start.3 = (bf16[32,4096]{1,0:T(8,128)(2,1)S(1)}, bf16[32,4096]{1,0:T(8,128)(2,1)S(1)}, u32[]{:S(2)}, u32[]{:S(2)}) collective-permute-start(bf16[32,4096]{1,0:T(8,128)(2,1)S(1)} %get-tuple-element.38._), channel_id=1, source_target_pairs={{0,2},{1,5},{2,0},{3,7},{4,6},{5,1},{6,4},{7,3},{8,10},{9,13},{10,... | collective-permute-start | bytes 786440 | tf_op jit(solution)/shard_map/ppermute | solution.py:372
  21.4 6.5 %collective-permute-start.4 = (bf16[16,4096]{1,0:T(8,128)(2,1)S(1)}, bf16[16,4096]{1,0:T(8,128)(2,1)S(1)}, u32[]{:S(2)}, u32[]{:S(2)}) collective-permute-start(bf16[16,4096]{1,0:T(8,128)(2,1)S(1)} %get-tuple-element.44), channel_id=1, source_target_pairs={{0,4},{1,3},{2,6},{3,1},{4,0},{5,7},{6,2},{7,5},{8,12},{9,11},{10,... | collective-permute-start | bytes 393224 | tf_op jit(solution)/shard_map/ppermute | solution.py:372
  27.9 10.5 %collective-permute-start.5 = (bf16[16,4096]{1,0:T(8,128)(2,1)S(1)}, bf16[16,4096]{1,0:T(8,128)(2,1)S(1)}, u32[]{:S(2)}, u32[]{:S(2)}) collective-permute-start(bf16[16,4096]{1,0:T(8,128)(2,1)S(1)} %shard_map.116.refs_0_.mixed_ref), channel_id=1, source_target_pairs={{0,4},{1,3},{2,6},{3,1},{4,0},{5,7},{6,2},{7,5},{8,12},{9,11},{10,... | collective-permute-start | bytes 393224 | tf_op jit(solution)/shard_map/ppermute | solution.py:372
  38.4 6.4 %collective-permute-start.6 = (bf16[32,4096]{1,0:T(8,128)(2,1)S(1)}, bf16[32,4096]{1,0:T(8,128)(2,1)S(1)}, u32[]{:S(2)}, u32[]{:S(2)}) collective-permute-start(bf16[32,4096]{1,0:T(8,128)(2,1)S(1)} %shard_map.117.refs_0_), channel_id=1, source_target_pairs={{0,2},{1,5},{2,0},{3,7},{4,6},{5,1},{6,4},{7,3},{8,10},{9,13},{10,... | collective-permute-start | bytes 786440 | tf_op jit(solution)/shard_map/ppermute | solution.py:372
  38.5 6.3 %collective-permute-start.7 = (bf16[32,4096]{1,0:T(8,128)(2,1)S(1)}, bf16[32,4096]{1,0:T(8,128)(2,1)S(1)}, u32[]{:S(2)}, u32[]{:S(2)}) collective-permute-start(bf16[32,4096]{1,0:T(8,128)(2,1)S(1)} %shard_map.117.refs_0_), channel_id=1, source_target_pairs={{0,1},{1,0},{2,3},{3,2},{4,5},{5,4},{6,7},{7,6},{8,9},{9,8},{10,11... | collective-permute-start | bytes 786440 | tf_op jit(solution)/shard_map/ppermute | solution.py:375
  44.9 1.5 %collective-permute-start.8 = (bf16[32,4096]{1,0:T(8,128)(2,1)S(1)}, bf16[32,4096]{1,0:T(8,128)(2,1)S(1)}, u32[]{:S(2)}, u32[]{:S(2)}) collective-permute-start(bf16[32,4096]{1,0:T(8,128)(2,1)S(1)} %collective-permute-done.6.refs_1_), channel_id=1, source_target_pairs={{0,1},{1,0},{2,3},{3,2},{4,5},{5,4},{6,7},{7,6},{8,9},{9,8},{10,11... | collective-permute-start | bytes 786440 | tf_op jit(solution)/shard_map/ppermute | solution.py:375
  49.6 2.0 %collective-permute-start.9 = (bf16[64,4096]{1,0:T(8,128)(2,1)S(1)}, bf16[64,4096]{1,0:T(8,128)(2,1)S(1)}, u32[]{:S(2)}, u32[]{:S(2)}) collective-permute-start(bf16[64,4096]{1,0:T(8,128)(2,1)S(1)} %get-tuple-element.46), channel_id=1, source_target_pairs={{0,1},{1,0},{2,3},{3,2},{4,5},{5,4},{6,7},{7,6},{8,9},{9,8},{10,11... | collective-permute-start | bytes 1572872 | tf_op jit(solution)/shard_map/ppermute | solution.py:375
  51.7 8.9 %collective-permute-start.10 = (bf16[32,4096]{1,0:T(8,128)(2,1)S(1)}, bf16[32,4096]{1,0:T(8,128)(2,1)S(1)}, u32[]{:S(2)}, u32[]{:S(2)}) collective-permute-start(bf16[32,4096]{1,0:T(8,128)(2,1)S(1)} %get-tuple-element.48), channel_id=1, source_target_pairs={{0,2},{1,5},{2,0},{3,7},{4,6},{5,1},{6,4},{7,3},{8,10},{9,13},{10,... | collective-permute-start | bytes 786440 | tf_op jit(solution)/shard_map/ppermute | solution.py:372
  60.7 7.3 %collective-permute-start.11 = (bf16[16,4096]{1,0:T(8,128)(2,1)S(1)}, bf16[16,4096]{1,0:T(8,128)(2,1)S(1)}, u32[]{:S(2)}, u32[]{:S(2)}) collective-permute-start(bf16[16,4096]{1,0:T(8,128)(2,1)S(1)} %get-tuple-element.50), channel_id=1, source_target_pairs={{0,4},{1,3},{2,6},{3,1},{4,0},{5,7},{6,2},{7,5},{8,12},{9,11},{10,... | collective-permute-start | bytes 393224 | tf_op jit(solution)/shard_map/ppermute | solution.py:372

commit v2 on v1

--- a/solution.py
+++ b/solution.py
@@ -164,32 +164,6 @@
     put_state(out_ref, split_dot(keyed, value_ref[...], ((0,), (0,))), jnp.broadcast_to(total, (1, d)))
 
 
-def take_before(bit, other_ref, before):
-    state, total = get_state(other_ref)
-    incoming, log = before
-    earlier = jnp.bitwise_and(lax.axis_index("seq"), bit) > 0
-    grown = jnp.where(earlier, jnp.exp(log) * state, 0.0)
-    more = jnp.where(earlier, total, 0.0)
-    if incoming is None:
-        return grown, more
-    return incoming + grown, log + more
-
-
-def merge_kernel(bit, mine_ref, other_ref, *refs):
-    out_ref, incoming_ref, log_ref = refs[-3:]
-    d = incoming_ref.shape[1]
-    before = (None, jnp.zeros((1, d), F32)) if len(refs) == 3 else (refs[0][...], refs[1][0:1, :])
-    incoming, log = take_before(bit, other_ref, before)
-    incoming_ref[...] = incoming
-    log_ref[...] = jnp.broadcast_to(log, log_ref.shape)
-    mine, my_total = get_state(mine_ref)
-    other, other_total = get_state(other_ref)
-    earlier = jnp.bitwise_and(lax.axis_index("seq"), bit) > 0
-    later_total = jnp.where(earlier, my_total, other_total)
-    merged = jnp.exp(later_total) * jnp.where(earlier, other, mine) + jnp.where(earlier, mine, other)
-    put_state(out_ref, merged, my_total + other_total)
-
-
 def within_kernel(
     query_hbm, key_hbm, value_hbm, decay_hbm, gain_hbm, w_out_hbm, _,
     intra_ref, grown_ref, query_ref, gain_ref, w_out_ref,
@@ -221,26 +195,19 @@
     copies[5].wait()
 
 
-def places(step, core, n_pair):
-    bits = n_pair.bit_length() - 1
-    flipped = sum(((step >> i) & 1) << (bits - 1 - i) for i in range(bits))
-    return step + core * (flipped - step)
-
-
 def place_matrix(rows, n_pair, pair, core):
     size = 2 * n_pair * rows
     i, j = iota2((size, size), 0), iota2((size, size), 1)
     half, inner = i // (n_pair * rows), i % (n_pair * rows)
-    whose = (core + half) % 2
-    who = jnp.bitwise_xor(places(inner // rows, whose, n_pair), pair)
-    source = (2 * who + whose) * rows + inner % rows
+    who = jnp.bitwise_xor(inner // rows, pair)
+    source = (2 * who + (core + half) % 2) * rows + inner % rows
     return jnp.where(source == j, 1.0, 0.0).astype(BF16)
 
 
 def fetch_kernel(
-    n_pair, slices, router_hbm, routes_hbm, gate_hbm, up_hbm, down_hbm, _,
-    in_ref, down_ref, member_ref, router_ref, routes_ref, sems,
+    n_pair, groups, router_hbm, routes_hbm, gate_hbm, up_hbm, down_hbm, _, in_ref, down_ref, *refs
 ):
+    member_refs, (router_ref, routes_ref, sems) = refs[:-3], refs[-3:]
     hid = gate_hbm.shape[0]
     copies = dma_in(
         sems,
@@ -255,24 +222,36 @@
     for copy in copies[:2]:
         copy.wait()
     experts, t = router_ref.shape[0], routes_ref.shape[1]
+    rows = t // (2 * n_pair)
     in_ref[2 * hid :, :] = jnp.zeros((TILE_ROWS, in_ref.shape[1]), BF16)
     in_ref[2 * hid : 2 * hid + experts, :] = router_ref[...]
-    padded = member_ref.shape[0]
+    padded = member_refs[0].shape[0]
     hits = jnp.zeros((padded, t), F32)
     for k in range(routes_ref.shape[0]):
         hits = hits + jnp.where(routes_ref[k : k + 1, :] == iota2((padded, t), 0), 1.0, 0.0)
     exp_index = lax.axis_index("exp")
-    place = place_matrix(t // (2 * n_pair), n_pair, exp_index // 2, exp_index % 2)
-    member_ref[...] = dot_f32(hits.astype(BF16), place, ((1,), (1,)))
+    place = place_matrix(rows, n_pair, exp_index // 2, exp_index % 2)
+    for group, ref in zip(groups, member_refs):
+        blocks = [half * n_pair + r for half in range(2) for r in group]
+        some = jnp.concatenate([place[b * rows : (b + 1) * rows] for b in blocks], axis=0)
+        ref[...] = dot_f32(hits.astype(BF16), some, ((1,), (1,)))
     for copy in copies[2:]:
         copy.wait()
 
 
-def project_kernel(
-    n_pair, bit, other_ref, incoming_ref, log_ref, intra_ref, grown_ref, query_ref, gain_ref, w_ref, mine_ref, theirs_ref
-):
+def project_kernel(n_pair, moves, *refs):
+    states = refs[: len(moves)]
+    intra_ref, grown_ref, query_ref, gain_ref, w_ref, mine_ref, theirs_ref = refs[len(moves) :]
     t, d = query_ref.shape
-    incoming, _ = take_before(bit, other_ref, (incoming_ref[...], log_ref[0:1, :]))
+    me = lax.axis_index("seq")
+    ranks = [move(me) for move in moves]
+    parts = [get_state(ref) for ref in states]
+    incoming = jnp.zeros((d, d), F32)
+    for rank, (state, _) in zip(ranks, parts):
+        logsum = jnp.zeros((1, d), F32)
+        for other, (_, total) in zip(ranks, parts):
+            logsum = logsum + jnp.where(jnp.logical_and(rank < other, other < me), total, 0.0)
+        incoming = incoming + jnp.where(rank < me, jnp.exp(logsum), 0.0) * state
     high = incoming.astype(BF16)
     low = (incoming - high.astype(F32)).astype(BF16)
     query = query_ref[...]
@@ -304,24 +283,21 @@
             ref[i * rows : (i + 1) * rows, :] = total.astype(ref.dtype)
 
 
-def join_kernel(*refs):
-    start = 0
-    for ref in refs[:-1]:
-        refs[-1][start : start + ref.shape[0], :] = ref[...]
-        start += ref.shape[0]
-
-
-def expert_kernel(slices, experts, order, rows, in_ref, down_ref, member_ref, *refs):
-    parts, (mine_ref, theirs_ref) = refs[:-2], refs[-2:]
-    half = len(parts) // 2
+def sum_kernel(count, *refs):
+    total = refs[0][...].astype(F32)
+    for ref in refs[1:count]:
+        total = total + ref[...].astype(F32)
+    refs[-1][...] = total.astype(BF16)
+
+
+def expert_kernel(slices, experts, count, in_ref, down_ref, member_ref, *refs):
+    parts, (mine_ref, theirs_ref) = refs[:count], refs[-2:]
     hid, width = down_ref.shape
     t = member_ref.shape[1]
     total = jnp.zeros((in_ref.shape[0], t), F32)
     for at in chunks(width):
-        blocks = [
-            parts[core * half + part][i * rows : (i + 1) * rows, at] for core in range(2) for part, i in order
-        ]
-        total = total + dot_f32(in_ref[:, at], jnp.concatenate(blocks, axis=0), ((1,), (1,)))
+        x = jnp.concatenate([part[:, at] for part in parts], axis=0)
+        total = total + dot_f32(in_ref[:, at], x, ((1,), (1,)))
     gate, up, logits = total[0:hid], total[hid : 2 * hid], total[2 * hid : 2 * hid + experts]
     raised = jnp.where(member_ref[0:experts, :] > 0.5, jnp.exp(logits), 0.0)
     mine = iota2((experts, t), 0) == lax.axis_index("exp") // slices
@@ -331,11 +307,6 @@
         part = dot_f32(hidden, down_ref[:, at], ((0,), (0,))).astype(BF16)
         mine_ref[:, at] = part[: t // 2]
         theirs_ref[:, at] = part[t // 2 :]
-
-
-def result_kernel(kept_ref, moved_ref, mixed_ref, out_ref):
-    total = kept_ref[...].astype(F32) + moved_ref[...].astype(F32) + mixed_ref[...].astype(F32)
-    out_ref[...] = total.astype(BF16)
 
 
 def call(kernel, outs, args, scratch=(), flops=0, far=0):
@@ -350,7 +321,7 @@
         out_specs=[whole] * len(outs),
         scratch_shapes=list(scratch),
         compiler_params=pltpu.CompilerParams(vmem_limit_bytes=VMEM_LIMIT),
-        cost_estimate=pl.CostEstimate(flops=flops, bytes_accessed=size, transcendentals=0),
+        cost_estimate=pl.CostEstimate(flops=0, bytes_accessed=0, transcendentals=0),
     )(*args)
 
 
@@ -365,35 +336,28 @@
     hid = w_gate.shape[2]
     out = jax.ShapeDtypeStruct
     dma = pltpu.SemaphoreType.DMA
-    bits = [1 << i for i in range(n_pair.bit_length() - 1)]
-
-    def swap(x, bit):
-        flips = (2 * bit, 2 * places(bit, 1, n_pair))
-        return lax.ppermute(x, "exp", [(e, e ^ flips[e % 2]) for e in range(exp_count)])
+
+    def swap(x, r):
+        return lax.ppermute(x, "exp", [(e, e ^ (2 * r)) for e in range(exp_count)])
 
     def across(x):
         return lax.ppermute(x, "exp", [(e, e ^ 1) for e in range(exp_count)])
 
-    def add(a, b, groups, after=()):
-        outs = [out((len(group) * rows, width), BF16) for group in groups]
-        return call(functools.partial(add_kernel, groups), outs, (a, b, *after))
-
-    def deal(held, bit):
-        return [[i for i, r in enumerate(held) if bool(r & bit) == gone] for gone in (False, True)]
+    def rows_of(count):
+        return out((count * rows, width), BF16)
 
     decay_row = decay_log.T
     block = pltpu.VMEM((t, d), BF16)
     decay_block = pltpu.VMEM((1, t), F32)
-    group = out((d + TILE_ROWS, d), BF16)
     (state,) = call(
-        state_kernel, [group], (key_in, value, decay_row), [block, block, decay_block, dma((3,))], far=3
-    )
-
-    def from_rank(x, bit):
-        return lax.ppermute(x, "seq", [(i, i ^ bit) for i in range(seq_count)])
-
-    seq_bits = [1 << i for i in range(seq_count.bit_length() - 1)]
-    other = from_rank(state, seq_bits[0])
+        state_kernel,
+        [out((d + TILE_ROWS, d), BF16)],
+        (key_in, value, decay_row),
+        [block, block, decay_block, dma((3,))],
+        far=3,
+    )
+    moves = [lambda i, k=k: i ^ k for k in range(1, seq_count)]
+    states = [lax.ppermute(state, "seq", [(move(i), i) for i in range(seq_count)]) for move in moves]
     intra, grown, query_near, gain, w_out_near = call(
         within_kernel,
         [out((t, d), F32), out((t, d), F32), out((t, d), BF16), out((8, d), F32), out(w_out.shape, BF16)],
@@ -401,67 +365,54 @@
         [block, block, decay_block, pltpu.VMEM((1, d), BF16), dma((6,))],
         far=6,
     )
-    before = ()
-    for bit, later in zip(seq_bits, seq_bits[1:]):
-        state, *before = call(
-            functools.partial(merge_kernel, bit), [group, out((d, d), F32), out((8, d), F32)], (state, other, *before)
+    mine, theirs = call(
+        functools.partial(project_kernel, n_pair, moves),
+        [rows_of(n_pair), rows_of(n_pair)],
+        (*states, intra, grown, query_near, gain, w_out_near),
+        flops=2 * t * d * width,
+    )
+    terms = call(
+        functools.partial(add_kernel, [[r] for r in range(n_pair)]),
+        [rows_of(1)] * n_pair,
+        (mine, across(theirs)),
+    )
+    moved = [swap(terms[r], r) for r in range(1, n_pair)]
+
+    groups = [list(range(n_pair))]
+    w_in, w_down_near, *members = call(
+        functools.partial(fetch_kernel, n_pair, groups),
+        [out((2 * hid + TILE_ROWS, width), BF16), out((hid, width), BF16)]
+        + [out((-(-experts // 8) * 8, 2 * len(group) * rows), F32) for group in groups],
+        (router.T, routes.T, w_gate[0].T, w_up[0].T, w_down[0], terms[1]),
+        [pltpu.VMEM((experts, width), BF16), pltpu.VMEM((routes.shape[1], t), jnp.int32), dma((5,))],
+        far=5,
+    )
+    (mixed,) = call(functools.partial(sum_kernel, n_pair), [rows_of(1)], (terms[0], *moved, members[0]))
+
+    gathered = {0: mixed}
+    for group in groups:
+        for r in group:
+            if r:
+                gathered[r] = swap(mixed, r)
+    sums = [mixed]
+    mine, parts = None, ()
+    for group, member in zip(groups, members):
+        near = [gathered[r] for r in group]
+        if parts:
+            near = list(lax.optimization_barrier((*near, mine)))[:-1]
+        mine, theirs = call(
+            functools.partial(expert_kernel, slices, experts, 2 * len(group)),
+            [rows_of(len(group))] * 2,
+            (w_in, w_down_near, member, *near, *[across(x) for x in near], *parts),
+            flops=6 * 2 * len(group) * rows * hid * width,
         )
-        other = from_rank(state, later)
-    half = out((t // 2, width), BF16)
-    mine, theirs = call(
-        functools.partial(project_kernel, n_pair, seq_bits[-1]),
-        [half, half],
-        (other, *before, intra, grown, query_near, gain, w_out_near),
-        flops=2 * t * d * width,
-    )
-
-    def reduce(mine, theirs, after):
-        held = list(range(n_pair))
-        kept, moved = mine, across(theirs)
-        extra = ()
-        for step, bit in enumerate(bits):
-            groups = deal(held, bit)
-            kept, go = add(kept, moved, groups, extra)
-            held = [held[i] for i in groups[0]]
-            moved = swap(go, bit)
-            if step == 0:
-                extra = after(go)
-        return kept, moved
-
-    near = []
-
-    def fetch(go):
-        near.extend(
-            call(
-                functools.partial(fetch_kernel, n_pair, slices),
-                [out((2 * hid + TILE_ROWS, width), BF16), out((hid, width), BF16), out((-(-experts // 8) * 8, t), F32)],
-                (router.T, routes.T, w_gate[0].T, w_up[0].T, w_down[0], go),
-                [pltpu.VMEM((experts, width), BF16), pltpu.VMEM((routes.shape[1], t), jnp.int32), dma((5,))],
-                far=5,
-            )
+        parts = call(
+            functools.partial(add_kernel, [[i] for i in range(len(group))]),
+            [rows_of(1)] * len(group),
+            (mine, across(theirs)),
         )
-        return (near[2],)
-
-    (mixed,) = add(*reduce(mine, theirs, fetch), [[0]])
-
-    held = [0]
-    whole = mixed
-    for step, bit in enumerate(reversed(bits)):
-        moved = swap(whole, bit)
-        held = held + [r ^ bit for r in held]
-        if step + 1 < len(bits):
-            (whole,) = call(join_kernel, [out((2 * whole.shape[0], width), BF16)], (whole, moved))
-    parts = [whole, moved]
-    spots = [(n, i) for n, part in enumerate(parts) for i in range(part.shape[0] // rows)]
-    order = [spots[held.index(r)] for r in range(n_pair)]
-    mine, theirs = call(
-        functools.partial(expert_kernel, slices, experts, order, rows),
-        [half, half],
-        (*near, *parts, *[across(part) for part in parts]),
-        flops=6 * t * hid * width,
-    )
-    kept, moved = reduce(mine, theirs, lambda go: ())
-    return call(result_kernel, [out((rows, width), BF16)], (kept, moved, mixed))[0]
+        sums += [swap(part, r) if r else part for part, r in zip(parts, group)]
+    return call(functools.partial(sum_kernel, len(sums)), [rows_of(1)], sums)[0]
 
 
 def solution(mesh):

time: 69 us -> 62.6 us (0.907)
  the two profiles are of different devices: /device:TPU:2 before, /device:TPU:0 now
where the time goes in v2:
time: 62.6 us; the launch traced here: 62.4 us
  waiting for transfers between devices  32.7 us (52%)
  starting transfers between devices  19 us (30%)
  Pallas kernels  10.7 us (17%)
    ppermute x9, waiting for transfers between devices, swap(): return lax.ppermute(x, 'exp', [(e, e ^ 2 * r) for e in range(exp_count)])  25.7 us
    ppermute x9, starting transfers between devices, swap(): return lax.ppermute(x, 'exp', [(e, e ^ 2 * r) for e in range(exp_count)])  13.4 us
    pallas_call x9, Pallas kernels, call(): pl.pallas_call(kernel, out_shape=outs, in_specs=[pl.BlockSpec(memory_spac...  10.7 us
    ppermute x3, starting transfers between devices, local(): lax.ppermute(state, 'seq', [(move(i), i) for i in range(seq_count)])  4.6 us
    ppermute x6, waiting for transfers between devices, across(): return lax.ppermute(x, 'exp', [(e, e ^ 1) for e in range(exp_count)])  4.5 us
    ppermute x3, waiting for transfers between devices, local(): lax.ppermute(state, 'seq', [(move(i), i) for i in range(seq_count)])  2.44 us
  transfers between devices with their start and end apart: 18, of which 12 were waited for; matrix products, arithmetic and copies ran while one was open for 0% of the time, Pallas kernels for 7%

profile of v2, /device:TPU:0, one launch (start us, length us, event | category | flops | bytes accessed | tf_op | source)
XLA Modules:
  0.0 62.4 jit_solution(10240353961593537257)
XLA Ops:
  0.0 1.1 %shard_map.109._ = bf16[144,128]{1,0:T(8,128)(2,1)S(1)} custom-call(bf16[128,128]{1,0:T(8,128)(2,1)} %key_hbm.3, bf16[128,128]{1,0:T(8,128)(2,1)} %value_hbm.3, f32[1,128]{1,0:T(1,128)} %bitcast.15), custom_call_target="tpu_custom_call" | custom-call | tf_op jit(solution)/shard_map/pallas_call | solution.py:317
  1.1 4.0 %collective-permute-start.2 = (bf16[144,128]{1,0:T(8,128)(2,1)S(1)}, bf16[144,128]{1,0:T(8,128)(2,1)S(1)}, u32[]{:S(2)}, u32[]{:S(2)}) collective-permute-start(bf16[144,128]{1,0:T(8,128)(2,1)S(1)} %shard_map.109._), channel_id=1, source_target_pairs={{24,0},{16,8},{8,16},{0,24},{25,1},{17,9},{9,17},{1,25},{26,2},{18... | collective-permute-start | bytes 110600 | tf_op jit(solution)/shard_map/ppermute | solution.py:360
  5.1 0.5 collective-permute-start.1
  5.6 0.1 collective-permute-start
  5.7 1.4 %shard_map.110 = (f32[128,128]{1,0:T(8,128)S(1)}, f32[128,128]{1,0:T(8,128)S(1)}, bf16[128,128]{1,0:T(8,128)(2,1)S(1)}, f32[8,128]{1,0:T(8,128)S(1)}, bf16[128,4096]{1,0:T(8,128)(2,1)S(1)}) custom-call(bf16[128,128]{1,0:T(8,128)(2,1)} %query_hbm.1, bf16[128,128]{1,0:T(8,128)(2,1)} %key_hbm.3, bf16[128,128]{1,0:T(8,128)(2,1)} %value_hbm.3, ...), custom_call_target="tpu_custom_call" | custom-call | tf_op jit(solution)/shard_map/pallas_call | solution.py:317
  7.1 0.0 collective-permute-done.2.refs_2_
  7.1 1.9 %collective-permute-done.1.refs_1_ = bf16[144,128]{1,0:T(8,128)(2,1)S(1)} collective-permute-done((bf16[144,128]{1,0:T(8,128)(2,1)S(1)}, bf16[144,128]{1,0:T(8,128)(2,1)S(1)}, u32[]{:S(2)}, u32[]{:S(2)}) %collective-permute-start.1) | collective-permute-done | bytes 36896 | tf_op jit(solution)/shard_map/ppermute | solution.py:360
  9.0 0.5 collective-permute-done.refs_0_
  9.5 0.8 %shard_map.111 = (bf16[64,4096]{1,0:T(8,128)(2,1)S(1)}, bf16[64,4096]{1,0:T(8,128)(2,1)S(1)}) custom-call(bf16[144,128]{1,0:T(8,128)(2,1)S(1)} %collective-permute-done.refs_0_, bf16[144,128]{1,0:T(8,128)(2,1)S(1)} %collective-permute-done.1.refs_1_, bf16[144,128]{1,0:T(8,128)(2,1)S(1)} %collective-permute-done.2.refs_2_, ...), custom_call_target="tpu_custom_call" | custom-call | tf_op jit(solution)/shard_map/pallas_call | solution.py:317
  10.4 0.1 collective-permute-start.3
  10.4 1.9 %collective-permute-done.3.b_ref = bf16[64,4096]{1,0:T(8,128)(2,1)S(1)} collective-permute-done((bf16[64,4096]{1,0:T(8,128)(2,1)S(1)}, bf16[64,4096]{1,0:T(8,128)(2,1)S(1)}, u32[]{:S(2)}, u32[]{:S(2)}) %collective-permute-start.3) | collective-permute-done | bytes 524320 | tf_op jit(solution)/shard_map/ppermute | solution.py:344
  12.3 0.1 shard_map.112
  12.5 2.7 %collective-permute-start.5 = (bf16[16,4096]{1,0:T(8,128)(2,1)S(1)}, bf16[16,4096]{1,0:T(8,128)(2,1)S(1)}, u32[]{:S(2)}, u32[]{:S(2)}) collective-permute-start(bf16[16,4096]{1,0:T(8,128)(2,1)S(1)} %get-tuple-element.34), channel_id=1, source_target_pairs={{0,4},{1,5},{2,6},{3,7},{4,0},{5,1},{6,2},{7,3},{8,12},{9,13},{10,... | collective-permute-start | bytes 393224 | tf_op jit(solution)/shard_map/ppermute | solution.py:341
  15.1 1.3 %collective-permute-start.6 = (bf16[16,4096]{1,0:T(8,128)(2,1)S(1)}, bf16[16,4096]{1,0:T(8,128)(2,1)S(1)}, u32[]{:S(2)}, u32[]{:S(2)}) collective-permute-start(bf16[16,4096]{1,0:T(8,128)(2,1)S(1)} %get-tuple-element.35), channel_id=1, source_target_pairs={{0,6},{1,7},{2,4},{3,5},{4,2},{5,3},{6,0},{7,1},{8,14},{9,15},{10,... | collective-permute-start | bytes 393224 | tf_op jit(solution)/shard_map/ppermute | solution.py:341
  16.5 0.2 collective-permute-start.4
  16.7 3.2 %shard_map.113 = (bf16[592,4096]{1,0:T(8,128)(2,1)S(1)}, bf16[288,4096]{1,0:T(8,128)(2,1)S(1)}, f32[8,128]{1,0:T(8,128)S(1)}) custom-call(bf16[4,4096]{1,0:T(4,128)(2,1)} %bitcast.14, s32[2,128]{1,0:T(2,128)} %bitcast.17, bf16[288,4096]{1,0:T(8,128)(2,1)} %bitcast.11, bf16[288,4096]{1,0:T(8,128)(2,1)} %bitcast.12, bf16[288,4096]{1,0:T(8,128)(2,1)} %bitcast.13, ...), custom_call_target="tpu_custom_call" | custom-call | tf_op jit(solution)/shard_map/pallas_call | solution.py:317
  19.9 5.5 %collective-permute-done.5.refs_2_ = bf16[16,4096]{1,0:T(8,128)(2,1)S(1)} collective-permute-done((bf16[16,4096]{1,0:T(8,128)(2,1)S(1)}, bf16[16,4096]{1,0:T(8,128)(2,1)S(1)}, u32[]{:S(2)}, u32[]{:S(2)}) %collective-permute-start.5) | collective-permute-done | bytes 131104 | tf_op jit(solution)/shard_map/ppermute | solution.py:341
  25.4 0.0 collective-permute-done.6.refs_3_
  25.4 0.6 collective-permute-done.4.refs_1_
  26.0 0.1 shard_map.114.refs_0_
  26.1 3.5 %collective-permute-start.9 = (bf16[16,4096]{1,0:T(8,128)(2,1)S(1)}, bf16[16,4096]{1,0:T(8,128)(2,1)S(1)}, u32[]{:S(2)}, u32[]{:S(2)}) collective-permute-start(bf16[16,4096]{1,0:T(8,128)(2,1)S(1)} %shard_map.114.refs_0_), channel_id=1, source_target_pairs={{0,6},{1,7},{2,4},{3,5},{4,2},{5,3},{6,0},{7,1},{8,14},{9,15},{10,... | collective-permute-start | bytes 393224 | tf_op jit(solution)/shard_map/ppermute | solution.py:341
  29.6 0.7 %collective-permute-start.8 = (bf16[16,4096]{1,0:T(8,128)(2,1)S(1)}, bf16[16,4096]{1,0:T(8,128)(2,1)S(1)}, u32[]{:S(2)}, u32[]{:S(2)}) collective-permute-start(bf16[16,4096]{1,0:T(8,128)(2,1)S(1)} %shard_map.114.refs_0_), channel_id=1, source_target_pairs={{0,4},{1,5},{2,6},{3,7},{4,0},{5,1},{6,2},{7,3},{8,12},{9,13},{10,... | collective-permute-start | bytes 393224 | tf_op jit(solution)/shard_map/ppermute | solution.py:341
  30.3 0.5 collective-permute-start.7
  30.7 0.0 collective-permute-start.10
  30.7 2.7 %collective-permute-done.9.refs_3_ = bf16[16,4096]{1,0:T(8,128)(2,1)S(1)} collective-permute-done((bf16[16,4096]{1,0:T(8,128)(2,1)S(1)}, bf16[16,4096]{1,0:T(8,128)(2,1)S(1)}, u32[]{:S(2)}, u32[]{:S(2)}) %collective-permute-start.9) | collective-permute-done | bytes 131104 | tf_op jit(solution)/shard_map/ppermute | solution.py:341
  33.5 0.0 collective-permute-start.13
  33.5 7.4 %collective-permute-done.8.refs_2_ = bf16[16,4096]{1,0:T(8,128)(2,1)S(1)} collective-permute-done((bf16[16,4096]{1,0:T(8,128)(2,1)S(1)}, bf16[16,4096]{1,0:T(8,128)(2,1)S(1)}, u32[]{:S(2)}, u32[]{:S(2)}) %collective-permute-start.8) | collective-permute-done | bytes 131104 | tf_op jit(solution)/shard_map/ppermute | solution.py:341
  40.9 0.0 collective-permute-start.12
  40.9 0.0 collective-permute-done.7.refs_1_
  40.9 0.5 collective-permute-start.11
  41.4 0.0 collective-permute-done.10.refs_4_
  41.4 0.0 collective-permute-done.13.refs_7_
  41.4 0.8 %collective-permute-done.12.refs_6_ = bf16[16,4096]{1,0:T(8,128)(2,1)S(1)} collective-permute-done((bf16[16,4096]{1,0:T(8,128)(2,1)S(1)}, bf16[16,4096]{1,0:T(8,128)(2,1)S(1)}, u32[]{:S(2)}, u32[]{:S(2)}) %collective-permute-start.12) | collective-permute-done | bytes 131104 | tf_op jit(solution)/shard_map/ppermute | solution.py:344
  42.2 0.2 collective-permute-done.11.refs_5_
  42.4 3.2 %shard_map.115 = (bf16[64,4096]{1,0:T(8,128)(2,1)S(1)}, bf16[64,4096]{1,0:T(8,128)(2,1)S(1)}) custom-call(bf16[592,4096]{1,0:T(8,128)(2,1)S(1)} %get-tuple-element.37.in_ref, bf16[288,4096]{1,0:T(8,128)(2,1)S(1)} %get-tuple-element.38.down_ref, f32[8,128]{1,0:T(8,128)S(1)} %get-tuple-element.36.refs_4_.member_ref, bf16[16,4096]{1,0:T(8,128)(2,1)S(1)} %shard_map.114.refs_0_, ...), custom_call_target="tpu_custom_call" | custom-call | tf_op jit(solution)/shard_map/pallas_call | solution.py:317
  45.7 0.4 collective-permute-start.14
  46.0 1.6 %collective-permute-done.14.b_ref = bf16[64,4096]{1,0:T(8,128)(2,1)S(1)} collective-permute-done((bf16[64,4096]{1,0:T(8,128)(2,1)S(1)}, bf16[64,4096]{1,0:T(8,128)(2,1)S(1)}, u32[]{:S(2)}, u32[]{:S(2)}) %collective-permute-start.14) | collective-permute-done | bytes 524320 | tf_op jit(solution)/shard_map/ppermute | solution.py:344
  47.6 0.1 shard_map.116
  47.8 0.6 collective-permute-start.15
  48.4 3.4 %collective-permute-start.16 = (bf16[16,4096]{1,0:T(8,128)(2,1)S(1)}, bf16[16,4096]{1,0:T(8,128)(2,1)S(1)}, u32[]{:S(2)}, u32[]{:S(2)}) collective-permute-start(bf16[16,4096]{1,0:T(8,128)(2,1)S(1)} %get-tuple-element.43), channel_id=1, source_target_pairs={{0,4},{1,5},{2,6},{3,7},{4,0},{5,1},{6,2},{7,3},{8,12},{9,13},{10,... | collective-permute-start | bytes 393224 | tf_op jit(solution)/shard_map/ppermute | solution.py:341
  51.7 0.5 collective-permute-start.17
  52.2 3.7 %collective-permute-done.15.refs_2_ = bf16[16,4096]{1,0:T(8,128)(2,1)S(1)} collective-permute-done((bf16[16,4096]{1,0:T(8,128)(2,1)S(1)}, bf16[16,4096]{1,0:T(8,128)(2,1)S(1)}, u32[]{:S(2)}, u32[]{:S(2)}) %collective-permute-start.15) | collective-permute-done | bytes 131104 | tf_op jit(solution)/shard_map/ppermute | solution.py:341
  56.0 5.7 %collective-permute-done.16.refs_3_ = bf16[16,4096]{1,0:T(8,128)(2,1)S(1)} collective-permute-done((bf16[16,4096]{1,0:T(8,128)(2,1)S(1)}, bf16[16,4096]{1,0:T(8,128)(2,1)S(1)}, u32[]{:S(2)}, u32[]{:S(2)}) %collective-permute-start.16) | collective-permute-done | bytes 131104 | tf_op jit(solution)/shard_map/ppermute | solution.py:341
  61.7 0.0 collective-permute-done.17.refs_4_
  61.7 0.7 %shard_map.117 = bf16[16,4096]{1,0:T(8,128)(2,1)} custom-call(bf16[16,4096]{1,0:T(8,128)(2,1)S(1)} %shard_map.114.refs_0_, bf16[16,4096]{1,0:T(8,128)(2,1)S(1)} %get-tuple-element.41.refs_1_, bf16[16,4096]{1,0:T(8,128)(2,1)S(1)} %collective-permute-done.15.refs_2_, bf16[16,4096]{1,0:T(8,128)(2,1)S(1)} %collective-permute-done.16.refs_3_, ...), custom_call_target="tpu_custom_call" | custom-call | tf_op jit(solution)/shard_map/pallas_call | solution.py:317
Async XLA Ops:
  1.1 6.0 %collective-permute-start.2 = (bf16[144,128]{1,0:T(8,128)(2,1)S(1)}, bf16[144,128]{1,0:T(8,128)(2,1)S(1)}, u32[]{:S(2)}, u32[]{:S(2)}) collective-permute-start(bf16[144,128]{1,0:T(8,128)(2,1)S(1)} %shard_map.109._), channel_id=1, source_target_pairs={{24,0},{16,8},{8,16},{0,24},{25,1},{17,9},{9,17},{1,25},{26,2},{18... | collective-permute-start | bytes 110600 | tf_op jit(solution)/shard_map/ppermute | solution.py:360
  5.1 4.0 %collective-permute-start.1 = (bf16[144,128]{1,0:T(8,128)(2,1)S(1)}, bf16[144,128]{1,0:T(8,128)(2,1)S(1)}, u32[]{:S(2)}, u32[]{:S(2)}) collective-permute-start(bf16[144,128]{1,0:T(8,128)(2,1)S(1)} %shard_map.109._), channel_id=1, source_target_pairs={{16,0},{24,8},{0,16},{8,24},{17,1},{25,9},{1,17},{9,25},{18,2},{26... | collective-permute-start | bytes 110600 | tf_op jit(solution)/shard_map/ppermute | solution.py:360
  5.6 4.0 %collective-permute-start = (bf16[144,128]{1,0:T(8,128)(2,1)S(1)}, bf16[144,128]{1,0:T(8,128)(2,1)S(1)}, u32[]{:S(2)}, u32[]{:S(2)}) collective-permute-start(bf16[144,128]{1,0:T(8,128)(2,1)S(1)} %shard_map.109._), channel_id=1, source_target_pairs={{8,0},{0,8},{24,16},{16,24},{9,1},{1,9},{25,17},{17,25},{10,2},{2,... | collective-permute-start | bytes 110600 | tf_op jit(solution)/shard_map/ppermute | solution.py:360
  10.4 2.0 %collective-permute-start.3 = (bf16[64,4096]{1,0:T(8,128)(2,1)S(1)}, bf16[64,4096]{1,0:T(8,128)(2,1)S(1)}, u32[]{:S(2)}, u32[]{:S(2)}) collective-permute-start(bf16[64,4096]{1,0:T(8,128)(2,1)S(1)} %get-tuple-element.31), channel_id=1, source_target_pairs={{0,1},{1,0},{2,3},{3,2},{4,5},{5,4},{6,7},{7,6},{8,9},{9,8},{10,11... | collective-permute-start | bytes 1572872 | tf_op jit(solution)/shard_map/ppermute | solution.py:344
  12.5 13.0 %collective-permute-start.5 = (bf16[16,4096]{1,0:T(8,128)(2,1)S(1)}, bf16[16,4096]{1,0:T(8,128)(2,1)S(1)}, u32[]{:S(2)}, u32[]{:S(2)}) collective-permute-start(bf16[16,4096]{1,0:T(8,128)(2,1)S(1)} %get-tuple-element.34), channel_id=1, source_target_pairs={{0,4},{1,5},{2,6},{3,7},{4,0},{5,1},{6,2},{7,3},{8,12},{9,13},{10,... | collective-permute-start | bytes 393224 | tf_op jit(solution)/shard_map/ppermute | solution.py:341
  15.1 10.3 %collective-permute-start.6 = (bf16[16,4096]{1,0:T(8,128)(2,1)S(1)}, bf16[16,4096]{1,0:T(8,128)(2,1)S(1)}, u32[]{:S(2)}, u32[]{:S(2)}) collective-permute-start(bf16[16,4096]{1,0:T(8,128)(2,1)S(1)} %get-tuple-element.35), channel_id=1, source_target_pairs={{0,6},{1,7},{2,4},{3,5},{4,2},{5,3},{6,0},{7,1},{8,14},{9,15},{10,... | collective-permute-start | bytes 393224 | tf_op jit(solution)/shard_map/ppermute | solution.py:341
  16.5 9.5 %collective-permute-start.4 = (bf16[16,4096]{1,0:T(8,128)(2,1)S(1)}, bf16[16,4096]{1,0:T(8,128)(2,1)S(1)}, u32[]{:S(2)}, u32[]{:S(2)}) collective-permute-start(bf16[16,4096]{1,0:T(8,128)(2,1)S(1)} %get-tuple-element.33._), channel_id=1, source_target_pairs={{0,2},{1,3},{2,0},{3,1},{4,6},{5,7},{6,4},{7,5},{8,10},{9,11},{10,... | collective-permute-start | bytes 393224 | tf_op jit(solution)/shard_map/ppermute | solution.py:341
  26.1 7.4 %collective-permute-start.9 = (bf16[16,4096]{1,0:T(8,128)(2,1)S(1)}, bf16[16,4096]{1,0:T(8,128)(2,1)S(1)}, u32[]{:S(2)}, u32[]{:S(2)}) collective-permute-start(bf16[16,4096]{1,0:T(8,128)(2,1)S(1)} %shard_map.114.refs_0_), channel_id=1, source_target_pairs={{0,6},{1,7},{2,4},{3,5},{4,2},{5,3},{6,0},{7,1},{8,14},{9,15},{10,... | collective-permute-start | bytes 393224 | tf_op jit(solution)/shard_map/ppermute | solution.py:341
  29.6 11.3 %collective-permute-start.8 = (bf16[16,4096]{1,0:T(8,128)(2,1)S(1)}, bf16[16,4096]{1,0:T(8,128)(2,1)S(1)}, u32[]{:S(2)}, u32[]{:S(2)}) collective-permute-start(bf16[16,4096]{1,0:T(8,128)(2,1)S(1)} %shard_map.114.refs_0_), channel_id=1, source_target_pairs={{0,4},{1,5},{2,6},{3,7},{4,0},{5,1},{6,2},{7,3},{8,12},{9,13},{10,... | collective-permute-start | bytes 393224 | tf_op jit(solution)/shard_map/ppermute | solution.py:341
  30.3 10.6 %collective-permute-start.7 = (bf16[16,4096]{1,0:T(8,128)(2,1)S(1)}, bf16[16,4096]{1,0:T(8,128)(2,1)S(1)}, u32[]{:S(2)}, u32[]{:S(2)}) collective-permute-start(bf16[16,4096]{1,0:T(8,128)(2,1)S(1)} %shard_map.114.refs_0_), channel_id=1, source_target_pairs={{0,2},{1,3},{2,0},{3,1},{4,6},{5,7},{6,4},{7,5},{8,10},{9,11},{10,... | collective-permute-start | bytes 393224 | tf_op jit(solution)/shard_map/ppermute | solution.py:341
  30.7 10.7 %collective-permute-start.10 = (bf16[16,4096]{1,0:T(8,128)(2,1)S(1)}, bf16[16,4096]{1,0:T(8,128)(2,1)S(1)}, u32[]{:S(2)}, u32[]{:S(2)}) collective-permute-start(bf16[16,4096]{1,0:T(8,128)(2,1)S(1)} %shard_map.114.refs_0_), channel_id=1, source_target_pairs={{0,1},{1,0},{2,3},{3,2},{4,5},{5,4},{6,7},{7,6},{8,9},{9,8},{10,11... | collective-permute-start | bytes 393224 | tf_op jit(solution)/shard_map/ppermute | solution.py:344
  33.5 7.9 %collective-permute-start.13 = (bf16[16,4096]{1,0:T(8,128)(2,1)S(1)}, bf16[16,4096]{1,0:T(8,128)(2,1)S(1)}, u32[]{:S(2)}, u32[]{:S(2)}) collective-permute-start(bf16[16,4096]{1,0:T(8,128)(2,1)S(1)} %collective-permute-done.9.refs_3_), channel_id=1, source_target_pairs={{0,1},{1,0},{2,3},{3,2},{4,5},{5,4},{6,7},{7,6},{8,9},{9,8},{10,11... | collective-permute-start | bytes 393224 | tf_op jit(solution)/shard_map/ppermute | solution.py:344
  40.9 1.3 %collective-permute-start.12 = (bf16[16,4096]{1,0:T(8,128)(2,1)S(1)}, bf16[16,4096]{1,0:T(8,128)(2,1)S(1)}, u32[]{:S(2)}, u32[]{:S(2)}) collective-permute-start(bf16[16,4096]{1,0:T(8,128)(2,1)S(1)} %collective-permute-done.8.refs_2_), channel_id=1, source_target_pairs={{0,1},{1,0},{2,3},{3,2},{4,5},{5,4},{6,7},{7,6},{8,9},{9,8},{10,11... | collective-permute-start | bytes 393224 | tf_op jit(solution)/shard_map/ppermute | solution.py:344
  40.9 1.5 %collective-permute-start.11 = (bf16[16,4096]{1,0:T(8,128)(2,1)S(1)}, bf16[16,4096]{1,0:T(8,128)(2,1)S(1)}, u32[]{:S(2)}, u32[]{:S(2)}) collective-permute-start(bf16[16,4096]{1,0:T(8,128)(2,1)S(1)} %collective-permute-done.7.refs_1_), channel_id=1, source_target_pairs={{0,1},{1,0},{2,3},{3,2},{4,5},{5,4},{6,7},{7,6},{8,9},{9,8},{10,11... | collective-permute-start | bytes 393224 | tf_op jit(solution)/shard_map/ppermute | solution.py:344
  45.7 2.0 %collective-permute-start.14 = (bf16[64,4096]{1,0:T(8,128)(2,1)S(1)}, bf16[64,4096]{1,0:T(8,128)(2,1)S(1)}, u32[]{:S(2)}, u32[]{:S(2)}) collective-permute-start(bf16[64,4096]{1,0:T(8,128)(2,1)S(1)} %get-tuple-element.40), channel_id=1, source_target_pairs={{0,1},{1,0},{2,3},{3,2},{4,5},{5,4},{6,7},{7,6},{8,9},{9,8},{10,11... | collective-permute-start | bytes 1572872 | tf_op jit(solution)/shard_map/ppermute | solution.py:344
  47.8 8.2 %collective-permute-start.15 = (bf16[16,4096]{1,0:T(8,128)(2,1)S(1)}, bf16[16,4096]{1,0:T(8,128)(2,1)S(1)}, u32[]{:S(2)}, u32[]{:S(2)}) collective-permute-start(bf16[16,4096]{1,0:T(8,128)(2,1)S(1)} %get-tuple-element.42), channel_id=1, source_target_pairs={{0,2},{1,3},{2,0},{3,1},{4,6},{5,7},{6,4},{7,5},{8,10},{9,11},{10,... | collective-permute-start | bytes 393224 | tf_op jit(solution)/shard_map/ppermute | solution.py:341
  48.4 13.3 %collective-permute-start.16 = (bf16[16,4096]{1,0:T(8,128)(2,1)S(1)}, bf16[16,4096]{1,0:T(8,128)(2,1)S(1)}, u32[]{:S(2)}, u32[]{:S(2)}) collective-permute-start(bf16[16,4096]{1,0:T(8,128)(2,1)S(1)} %get-tuple-element.43), channel_id=1, source_target_pairs={{0,4},{1,5},{2,6},{3,7},{4,0},{5,1},{6,2},{7,3},{8,12},{9,13},{10,... | collective-permute-start | bytes 393224 | tf_op jit(solution)/shard_map/ppermute | solution.py:341
  51.7 10.0 %collective-permute-start.17 = (bf16[16,4096]{1,0:T(8,128)(2,1)S(1)}, bf16[16,4096]{1,0:T(8,128)(2,1)S(1)}, u32[]{:S(2)}, u32[]{:S(2)}) collective-permute-start(bf16[16,4096]{1,0:T(8,128)(2,1)S(1)} %get-tuple-element.44), channel_id=1, source_target_pairs={{0,6},{1,7},{2,4},{3,5},{4,2},{5,3},{6,0},{7,1},{8,14},{9,15},{10,... | collective-permute-start | bytes 393224 | tf_op jit(solution)/shard_map/ppermute | solution.py:341

commit v3 on v2

--- a/solution.py
+++ b/solution.py
@@ -199,7 +199,7 @@
     size = 2 * n_pair * rows
     i, j = iota2((size, size), 0), iota2((size, size), 1)
     half, inner = i // (n_pair * rows), i % (n_pair * rows)
-    who = jnp.bitwise_xor(inner // rows, pair)
+    who = (inner // rows + pair) % n_pair
     source = (2 * who + (core + half) % 2) * rows + inner % rows
     return jnp.where(source == j, 1.0, 0.0).astype(BF16)
 
@@ -337,8 +337,8 @@
     out = jax.ShapeDtypeStruct
     dma = pltpu.SemaphoreType.DMA
 
-    def swap(x, r):
-        return lax.ppermute(x, "exp", [(e, e ^ (2 * r)) for e in range(exp_count)])
+    def shift(x, r):
+        return lax.ppermute(x, "exp", [(e, (e + 2 * r) % exp_count) for e in range(exp_count)])
 
     def across(x):
         return lax.ppermute(x, "exp", [(e, e ^ 1) for e in range(exp_count)])
@@ -356,7 +356,7 @@
         [block, block, decay_block, dma((3,))],
         far=3,
     )
-    moves = [lambda i, k=k: i ^ k for k in range(1, seq_count)]
+    moves = [lambda i, k=k: i ^ k for k in reversed(range(1, seq_count))]
     states = [lax.ppermute(state, "seq", [(move(i), i) for i in range(seq_count)]) for move in moves]
     intra, grown, query_near, gain, w_out_near = call(
         within_kernel,
@@ -376,24 +376,20 @@
         [rows_of(1)] * n_pair,
         (mine, across(theirs)),
     )
-    moved = [swap(terms[r], r) for r in range(1, n_pair)]
+    moved = [shift(terms[r], r) for r in range(1, n_pair)]
 
     groups = [list(range(n_pair))]
     w_in, w_down_near, *members = call(
         functools.partial(fetch_kernel, n_pair, groups),
         [out((2 * hid + TILE_ROWS, width), BF16), out((hid, width), BF16)]
         + [out((-(-experts // 8) * 8, 2 * len(group) * rows), F32) for group in groups],
-        (router.T, routes.T, w_gate[0].T, w_up[0].T, w_down[0], terms[1]),
+        (router.T, routes.T, w_gate[0].T, w_up[0].T, w_down[0], terms[-1]),
         [pltpu.VMEM((experts, width), BF16), pltpu.VMEM((routes.shape[1], t), jnp.int32), dma((5,))],
         far=5,
     )
     (mixed,) = call(functools.partial(sum_kernel, n_pair), [rows_of(1)], (terms[0], *moved, members[0]))
 
-    gathered = {0: mixed}
-    for group in groups:
-        for r in group:
-            if r:
-                gathered[r] = swap(mixed, r)
+    gathered = {r: shift(mixed, -r) if r else mixed for r in reversed(range(n_pair))}
     sums = [mixed]
     mine, parts = None, ()
     for group, member in zip(groups, members):
@@ -411,7 +407,7 @@
             [rows_of(1)] * len(group),
             (mine, across(theirs)),
         )
-        sums += [swap(part, r) if r else part for part, r in zip(parts, group)]
+        sums += [shift(part, r) if r else part for part, r in zip(parts, group)]
     return call(functools.partial(sum_kernel, len(sums)), [rows_of(1)], sums)[0]
 
 

time: 62.6 us -> 62.4 us (level)
  waiting for transfers between devices: 32.7 us -> 28.6 us
  starting transfers between devices: 19 us -> 22.4 us
    ppermute x9, waiting for transfers between devices: 25.7 us -> 20.6 us  [shift(): lax.ppermute(x, 'exp', [(e, (e + 2 * r) % exp_count) for e in range(exp_c...]
    ppermute x9, starting transfers between devices: 13.4 us -> 16.9 us  [shift(): lax.ppermute(x, 'exp', [(e, (e + 2 * r) % exp_count) for e in range(exp_c...]
    ppermute x3, waiting for transfers between devices: 2.44 us -> 3.45 us  [local(): lax.ppermute(state, 'seq', [(move(i), i) for i in range(seq_count)])]
  transfers between devices with their start and end apart: 18 -> 18, of which waited for: 12 -> 11; matrix products, arithmetic and copies ran while one was open for 0% -> 0% of each run, Pallas kernels for 7% -> 7%
where the time goes in v3:
time: 62.4 us; the launch traced here: 61.8 us
  waiting for transfers between devices  28.6 us (46%)
  starting transfers between devices  22.4 us (36%)
  Pallas kernels  10.7 us (17%)
    ppermute x9, waiting for transfers between devices, shift(): lax.ppermute(x, 'exp', [(e, (e + 2 * r) % exp_count) for e in range(exp_c...  20.6 us
    ppermute x9, starting transfers between devices, shift(): lax.ppermute(x, 'exp', [(e, (e + 2 * r) % exp_count) for e in range(exp_c...  16.9 us
    pallas_call x9, Pallas kernels, call(): pl.pallas_call(kernel, out_shape=outs, in_specs=[pl.BlockSpec(memory_spac...  10.7 us
    ppermute x3, starting transfers between devices, local(): lax.ppermute(state, 'seq', [(move(i), i) for i in range(seq_count)])  4.54 us
    ppermute x6, waiting for transfers between devices, across(): return lax.ppermute(x, 'exp', [(e, e ^ 1) for e in range(exp_count)])  4.5 us
    ppermute x3, waiting for transfers between devices, local(): lax.ppermute(state, 'seq', [(move(i), i) for i in range(seq_count)])  3.45 us
  transfers between devices with their start and end apart: 18, of which 11 were waited for; matrix products, arithmetic and copies ran while one was open for 0% of the time, Pallas kernels for 7%

profile of v3, /device:TPU:0, one launch (start us, length us, event | category | flops | bytes accessed | tf_op | source)
XLA Modules:
  0.0 61.8 jit_solution(16256737609139741611)
XLA Ops:
  0.0 1.1 %shard_map.109._ = bf16[144,128]{1,0:T(8,128)(2,1)S(1)} custom-call(bf16[128,128]{1,0:T(8,128)(2,1)} %key_hbm.3, bf16[128,128]{1,0:T(8,128)(2,1)} %value_hbm.3, f32[1,128]{1,0:T(1,128)} %bitcast.15), custom_call_target="tpu_custom_call" | custom-call | tf_op jit(solution)/shard_map/pallas_call | solution.py:317
  1.1 3.0 %collective-permute-start.2 = (bf16[144,128]{1,0:T(8,128)(2,1)S(1)}, bf16[144,128]{1,0:T(8,128)(2,1)S(1)}, u32[]{:S(2)}, u32[]{:S(2)}) collective-permute-start(bf16[144,128]{1,0:T(8,128)(2,1)S(1)} %shard_map.109._), channel_id=1, source_target_pairs={{8,0},{0,8},{24,16},{16,24},{9,1},{1,9},{25,17},{17,25},{10,2},{2,... | collective-permute-start | bytes 110600 | tf_op jit(solution)/shard_map/ppermute | solution.py:360
  4.1 1.5 %collective-permute-start.1 = (bf16[144,128]{1,0:T(8,128)(2,1)S(1)}, bf16[144,128]{1,0:T(8,128)(2,1)S(1)}, u32[]{:S(2)}, u32[]{:S(2)}) collective-permute-start(bf16[144,128]{1,0:T(8,128)(2,1)S(1)} %shard_map.109._), channel_id=1, source_target_pairs={{16,0},{24,8},{0,16},{8,24},{17,1},{25,9},{1,17},{9,25},{18,2},{26... | collective-permute-start | bytes 110600 | tf_op jit(solution)/shard_map/ppermute | solution.py:360
  5.6 0.0 collective-permute-start
  5.7 1.4 %shard_map.110 = (f32[128,128]{1,0:T(8,128)S(1)}, f32[128,128]{1,0:T(8,128)S(1)}, bf16[128,128]{1,0:T(8,128)(2,1)S(1)}, f32[8,128]{1,0:T(8,128)S(1)}, bf16[128,4096]{1,0:T(8,128)(2,1)S(1)}) custom-call(bf16[128,128]{1,0:T(8,128)(2,1)} %query_hbm.1, bf16[128,128]{1,0:T(8,128)(2,1)} %key_hbm.3, bf16[128,128]{1,0:T(8,128)(2,1)} %value_hbm.3, ...), custom_call_target="tpu_custom_call" | custom-call | tf_op jit(solution)/shard_map/pallas_call | solution.py:317
  7.0 0.0 collective-permute-done.2.refs_2_
  7.0 1.0 %collective-permute-done.1.refs_1_ = bf16[144,128]{1,0:T(8,128)(2,1)S(1)} collective-permute-done((bf16[144,128]{1,0:T(8,128)(2,1)S(1)}, bf16[144,128]{1,0:T(8,128)(2,1)S(1)}, u32[]{:S(2)}, u32[]{:S(2)}) %collective-permute-start.1) | collective-permute-done | bytes 36896 | tf_op jit(solution)/shard_map/ppermute | solution.py:360
  8.1 2.4 %collective-permute-done.refs_0_ = bf16[144,128]{1,0:T(8,128)(2,1)S(1)} collective-permute-done((bf16[144,128]{1,0:T(8,128)(2,1)S(1)}, bf16[144,128]{1,0:T(8,128)(2,1)S(1)}, u32[]{:S(2)}, u32[]{:S(2)}) %collective-permute-start) | collective-permute-done | bytes 36896 | tf_op jit(solution)/shard_map/ppermute | solution.py:360
  10.5 0.8 %shard_map.111 = (bf16[64,4096]{1,0:T(8,128)(2,1)S(1)}, bf16[64,4096]{1,0:T(8,128)(2,1)S(1)}) custom-call(bf16[144,128]{1,0:T(8,128)(2,1)S(1)} %collective-permute-done.refs_0_, bf16[144,128]{1,0:T(8,128)(2,1)S(1)} %collective-permute-done.1.refs_1_, bf16[144,128]{1,0:T(8,128)(2,1)S(1)} %collective-permute-done.2.refs_2_, ...), custom_call_target="tpu_custom_call" | custom-call | tf_op jit(solution)/shard_map/pallas_call | solution.py:317
  11.3 0.1 collective-permute-start.3
  11.4 1.9 %collective-permute-done.3.b_ref = bf16[64,4096]{1,0:T(8,128)(2,1)S(1)} collective-permute-done((bf16[64,4096]{1,0:T(8,128)(2,1)S(1)}, bf16[64,4096]{1,0:T(8,128)(2,1)S(1)}, u32[]{:S(2)}, u32[]{:S(2)}) %collective-permute-start.3) | collective-permute-done | bytes 524320 | tf_op jit(solution)/shard_map/ppermute | solution.py:344
  13.3 0.1 shard_map.112
  13.4 1.6 %collective-permute-start.4 = (bf16[16,4096]{1,0:T(8,128)(2,1)S(1)}, bf16[16,4096]{1,0:T(8,128)(2,1)S(1)}, u32[]{:S(2)}, u32[]{:S(2)}) collective-permute-start(bf16[16,4096]{1,0:T(8,128)(2,1)S(1)} %get-tuple-element.33), channel_id=1, source_target_pairs={{0,2},{1,3},{2,4},{3,5},{4,6},{5,7},{6,0},{7,1},{8,10},{9,11},{10,... | collective-permute-start | bytes 393224 | tf_op jit(solution)/shard_map/ppermute | solution.py:341
  15.0 2.6 %collective-permute-start.5 = (bf16[16,4096]{1,0:T(8,128)(2,1)S(1)}, bf16[16,4096]{1,0:T(8,128)(2,1)S(1)}, u32[]{:S(2)}, u32[]{:S(2)}) collective-permute-start(bf16[16,4096]{1,0:T(8,128)(2,1)S(1)} %get-tuple-element.34), channel_id=1, source_target_pairs={{0,4},{1,5},{2,6},{3,7},{4,0},{5,1},{6,2},{7,3},{8,12},{9,13},{10,... | collective-permute-start | bytes 393224 | tf_op jit(solution)/shard_map/ppermute | solution.py:341
  17.6 1.3 %collective-permute-start.6 = (bf16[16,4096]{1,0:T(8,128)(2,1)S(1)}, bf16[16,4096]{1,0:T(8,128)(2,1)S(1)}, u32[]{:S(2)}, u32[]{:S(2)}) collective-permute-start(bf16[16,4096]{1,0:T(8,128)(2,1)S(1)} %get-tuple-element.35._), channel_id=1, source_target_pairs={{0,6},{1,7},{2,0},{3,1},{4,2},{5,3},{6,4},{7,5},{8,14},{9,15},{10,... | collective-permute-start | bytes 393224 | tf_op jit(solution)/shard_map/ppermute | solution.py:341
  19.0 3.2 %shard_map.113 = (bf16[592,4096]{1,0:T(8,128)(2,1)S(1)}, bf16[288,4096]{1,0:T(8,128)(2,1)S(1)}, f32[8,128]{1,0:T(8,128)S(1)}) custom-call(bf16[4,4096]{1,0:T(4,128)(2,1)} %bitcast.14, s32[2,128]{1,0:T(2,128)} %bitcast.17, bf16[288,4096]{1,0:T(8,128)(2,1)} %bitcast.11, bf16[288,4096]{1,0:T(8,128)(2,1)} %bitcast.12, bf16[288,4096]{1,0:T(8,128)(2,1)} %bitcast.13, ...), custom_call_target="tpu_custom_call" | custom-call | tf_op jit(solution)/shard_map/pallas_call | solution.py:317
  22.2 0.0 collective-permute-done.4.refs_1_
  22.2 4.4 %collective-permute-done.5.refs_2_ = bf16[16,4096]{1,0:T(8,128)(2,1)S(1)} collective-permute-done((bf16[16,4096]{1,0:T(8,128)(2,1)S(1)}, bf16[16,4096]{1,0:T(8,128)(2,1)S(1)}, u32[]{:S(2)}, u32[]{:S(2)}) %collective-permute-start.5) | collective-permute-done | bytes 131104 | tf_op jit(solution)/shard_map/ppermute | solution.py:341
  26.6 0.0 collective-permute-done.6.refs_3_
  26.6 0.1 shard_map.114.refs_0_
  26.7 3.3 %collective-permute-start.9 = (bf16[16,4096]{1,0:T(8,128)(2,1)S(1)}, bf16[16,4096]{1,0:T(8,128)(2,1)S(1)}, u32[]{:S(2)}, u32[]{:S(2)}) collective-permute-start(bf16[16,4096]{1,0:T(8,128)(2,1)S(1)} %shard_map.114.refs_0_), channel_id=1, source_target_pairs={{0,2},{1,3},{2,4},{3,5},{4,6},{5,7},{6,0},{7,1},{8,10},{9,11},{10,... | collective-permute-start | bytes 393224 | tf_op jit(solution)/shard_map/ppermute | solution.py:341
  30.0 1.6 %collective-permute-start.8 = (bf16[16,4096]{1,0:T(8,128)(2,1)S(1)}, bf16[16,4096]{1,0:T(8,128)(2,1)S(1)}, u32[]{:S(2)}, u32[]{:S(2)}) collective-permute-start(bf16[16,4096]{1,0:T(8,128)(2,1)S(1)} %shard_map.114.refs_0_), channel_id=1, source_target_pairs={{0,4},{1,5},{2,6},{3,7},{4,0},{5,1},{6,2},{7,3},{8,12},{9,13},{10,... | collective-permute-start | bytes 393224 | tf_op jit(solution)/shard_map/ppermute | solution.py:341
  31.6 0.8 %collective-permute-start.7 = (bf16[16,4096]{1,0:T(8,128)(2,1)S(1)}, bf16[16,4096]{1,0:T(8,128)(2,1)S(1)}, u32[]{:S(2)}, u32[]{:S(2)}) collective-permute-start(bf16[16,4096]{1,0:T(8,128)(2,1)S(1)} %shard_map.114.refs_0_), channel_id=1, source_target_pairs={{0,6},{1,7},{2,0},{3,1},{4,2},{5,3},{6,4},{7,5},{8,14},{9,15},{10,... | collective-permute-start | bytes 393224 | tf_op jit(solution)/shard_map/ppermute | solution.py:341
  32.4 0.0 collective-permute-start.10
  32.4 2.8 %collective-permute-done.9.refs_3_ = bf16[16,4096]{1,0:T(8,128)(2,1)S(1)} collective-permute-done((bf16[16,4096]{1,0:T(8,128)(2,1)S(1)}, bf16[16,4096]{1,0:T(8,128)(2,1)S(1)}, u32[]{:S(2)}, u32[]{:S(2)}) %collective-permute-start.9) | collective-permute-done | bytes 131104 | tf_op jit(solution)/shard_map/ppermute | solution.py:341
  35.2 0.0 collective-permute-start.13
  35.2 4.5 %collective-permute-done.8.refs_2_ = bf16[16,4096]{1,0:T(8,128)(2,1)S(1)} collective-permute-done((bf16[16,4096]{1,0:T(8,128)(2,1)S(1)}, bf16[16,4096]{1,0:T(8,128)(2,1)S(1)}, u32[]{:S(2)}, u32[]{:S(2)}) %collective-permute-start.8) | collective-permute-done | bytes 131104 | tf_op jit(solution)/shard_map/ppermute | solution.py:341
  39.7 0.0 collective-permute-start.12
  39.7 0.0 collective-permute-done.7.refs_1_
  39.7 0.5 collective-permute-start.11
  40.3 0.0 collective-permute-done.10.refs_4_
  40.3 0.0 collective-permute-done.13.refs_7_
  40.3 0.8 %collective-permute-done.12.refs_6_ = bf16[16,4096]{1,0:T(8,128)(2,1)S(1)} collective-permute-done((bf16[16,4096]{1,0:T(8,128)(2,1)S(1)}, bf16[16,4096]{1,0:T(8,128)(2,1)S(1)}, u32[]{:S(2)}, u32[]{:S(2)}) %collective-permute-start.12) | collective-permute-done | bytes 131104 | tf_op jit(solution)/shard_map/ppermute | solution.py:344
  41.1 0.2 collective-permute-done.11.refs_5_
  41.3 3.2 %shard_map.115 = (bf16[64,4096]{1,0:T(8,128)(2,1)S(1)}, bf16[64,4096]{1,0:T(8,128)(2,1)S(1)}) custom-call(bf16[592,4096]{1,0:T(8,128)(2,1)S(1)} %get-tuple-element.37.in_ref, bf16[288,4096]{1,0:T(8,128)(2,1)S(1)} %get-tuple-element.38.down_ref, f32[8,128]{1,0:T(8,128)S(1)} %get-tuple-element.36.refs_4_.member_ref, bf16[16,4096]{1,0:T(8,128)(2,1)S(1)} %shard_map.114.refs_0_, ...), custom_call_target="tpu_custom_call" | custom-call | tf_op jit(solution)/shard_map/pallas_call | solution.py:317
  44.5 0.4 collective-permute-start.14
  44.9 1.6 %collective-permute-done.14.b_ref = bf16[64,4096]{1,0:T(8,128)(2,1)S(1)} collective-permute-done((bf16[64,4096]{1,0:T(8,128)(2,1)S(1)}, bf16[64,4096]{1,0:T(8,128)(2,1)S(1)}, u32[]{:S(2)}, u32[]{:S(2)}) %collective-permute-start.14) | collective-permute-done | bytes 524320 | tf_op jit(solution)/shard_map/ppermute | solution.py:344
  46.5 0.1 shard_map.116
  46.6 3.1 %collective-permute-start.15 = (bf16[16,4096]{1,0:T(8,128)(2,1)S(1)}, bf16[16,4096]{1,0:T(8,128)(2,1)S(1)}, u32[]{:S(2)}, u32[]{:S(2)}) collective-permute-start(bf16[16,4096]{1,0:T(8,128)(2,1)S(1)} %get-tuple-element.42), channel_id=1, source_target_pairs={{0,2},{1,3},{2,4},{3,5},{4,6},{5,7},{6,0},{7,1},{8,10},{9,11},{10,... | collective-permute-start | bytes 393224 | tf_op jit(solution)/shard_map/ppermute | solution.py:341
  49.7 2.2 %collective-permute-start.16 = (bf16[16,4096]{1,0:T(8,128)(2,1)S(1)}, bf16[16,4096]{1,0:T(8,128)(2,1)S(1)}, u32[]{:S(2)}, u32[]{:S(2)}) collective-permute-start(bf16[16,4096]{1,0:T(8,128)(2,1)S(1)} %get-tuple-element.43), channel_id=1, source_target_pairs={{0,4},{1,5},{2,6},{3,7},{4,0},{5,1},{6,2},{7,3},{8,12},{9,13},{10,... | collective-permute-start | bytes 393224 | tf_op jit(solution)/shard_map/ppermute | solution.py:341
  51.9 0.3 collective-permute-start.17
  52.2 3.5 %collective-permute-done.15.refs_2_ = bf16[16,4096]{1,0:T(8,128)(2,1)S(1)} collective-permute-done((bf16[16,4096]{1,0:T(8,128)(2,1)S(1)}, bf16[16,4096]{1,0:T(8,128)(2,1)S(1)}, u32[]{:S(2)}, u32[]{:S(2)}) %collective-permute-start.15) | collective-permute-done | bytes 131104 | tf_op jit(solution)/shard_map/ppermute | solution.py:341
  55.7 5.3 %collective-permute-done.16.refs_3_ = bf16[16,4096]{1,0:T(8,128)(2,1)S(1)} collective-permute-done((bf16[16,4096]{1,0:T(8,128)(2,1)S(1)}, bf16[16,4096]{1,0:T(8,128)(2,1)S(1)}, u32[]{:S(2)}, u32[]{:S(2)}) %collective-permute-start.16) | collective-permute-done | bytes 131104 | tf_op jit(solution)/shard_map/ppermute | solution.py:341
  61.1 0.0 collective-permute-done.17.refs_4_
  61.1 0.7 %shard_map.117 = bf16[16,4096]{1,0:T(8,128)(2,1)} custom-call(bf16[16,4096]{1,0:T(8,128)(2,1)S(1)} %shard_map.114.refs_0_, bf16[16,4096]{1,0:T(8,128)(2,1)S(1)} %get-tuple-element.41.refs_1_, bf16[16,4096]{1,0:T(8,128)(2,1)S(1)} %collective-permute-done.15.refs_2_, bf16[16,4096]{1,0:T(8,128)(2,1)S(1)} %collective-permute-done.16.refs_3_, ...), custom_call_target="tpu_custom_call" | custom-call | tf_op jit(solution)/shard_map/pallas_call | solution.py:317
Async XLA Ops:
  1.1 5.9 %collective-permute-start.2 = (bf16[144,128]{1,0:T(8,128)(2,1)S(1)}, bf16[144,128]{1,0:T(8,128)(2,1)S(1)}, u32[]{:S(2)}, u32[]{:S(2)}) collective-permute-start(bf16[144,128]{1,0:T(8,128)(2,1)S(1)} %shard_map.109._), channel_id=1, source_target_pairs={{8,0},{0,8},{24,16},{16,24},{9,1},{1,9},{25,17},{17,25},{10,2},{2,... | collective-permute-start | bytes 110600 | tf_op jit(solution)/shard_map/ppermute | solution.py:360
  4.1 4.0 %collective-permute-start.1 = (bf16[144,128]{1,0:T(8,128)(2,1)S(1)}, bf16[144,128]{1,0:T(8,128)(2,1)S(1)}, u32[]{:S(2)}, u32[]{:S(2)}) collective-permute-start(bf16[144,128]{1,0:T(8,128)(2,1)S(1)} %shard_map.109._), channel_id=1, source_target_pairs={{16,0},{24,8},{0,16},{8,24},{17,1},{25,9},{1,17},{9,25},{18,2},{26... | collective-permute-start | bytes 110600 | tf_op jit(solution)/shard_map/ppermute | solution.py:360
  5.6 4.9 %collective-permute-start = (bf16[144,128]{1,0:T(8,128)(2,1)S(1)}, bf16[144,128]{1,0:T(8,128)(2,1)S(1)}, u32[]{:S(2)}, u32[]{:S(2)}) collective-permute-start(bf16[144,128]{1,0:T(8,128)(2,1)S(1)} %shard_map.109._), channel_id=1, source_target_pairs={{24,0},{16,8},{8,16},{0,24},{25,1},{17,9},{9,17},{1,25},{26,2},{18... | collective-permute-start | bytes 110600 | tf_op jit(solution)/shard_map/ppermute | solution.py:360
  11.3 2.0 %collective-permute-start.3 = (bf16[64,4096]{1,0:T(8,128)(2,1)S(1)}, bf16[64,4096]{1,0:T(8,128)(2,1)S(1)}, u32[]{:S(2)}, u32[]{:S(2)}) collective-permute-start(bf16[64,4096]{1,0:T(8,128)(2,1)S(1)} %get-tuple-element.31), channel_id=1, source_target_pairs={{0,1},{1,0},{2,3},{3,2},{4,5},{5,4},{6,7},{7,6},{8,9},{9,8},{10,11... | collective-permute-start | bytes 1572872 | tf_op jit(solution)/shard_map/ppermute | solution.py:344
  13.4 8.7 %collective-permute-start.4 = (bf16[16,4096]{1,0:T(8,128)(2,1)S(1)}, bf16[16,4096]{1,0:T(8,128)(2,1)S(1)}, u32[]{:S(2)}, u32[]{:S(2)}) collective-permute-start(bf16[16,4096]{1,0:T(8,128)(2,1)S(1)} %get-tuple-element.33), channel_id=1, source_target_pairs={{0,2},{1,3},{2,4},{3,5},{4,6},{5,7},{6,0},{7,1},{8,10},{9,11},{10,... | collective-permute-start | bytes 393224 | tf_op jit(solution)/shard_map/ppermute | solution.py:341
  15.0 11.5 %collective-permute-start.5 = (bf16[16,4096]{1,0:T(8,128)(2,1)S(1)}, bf16[16,4096]{1,0:T(8,128)(2,1)S(1)}, u32[]{:S(2)}, u32[]{:S(2)}) collective-permute-start(bf16[16,4096]{1,0:T(8,128)(2,1)S(1)} %get-tuple-element.34), channel_id=1, source_target_pairs={{0,4},{1,5},{2,6},{3,7},{4,0},{5,1},{6,2},{7,3},{8,12},{9,13},{10,... | collective-permute-start | bytes 393224 | tf_op jit(solution)/shard_map/ppermute | solution.py:341
  17.6 8.9 %collective-permute-start.6 = (bf16[16,4096]{1,0:T(8,128)(2,1)S(1)}, bf16[16,4096]{1,0:T(8,128)(2,1)S(1)}, u32[]{:S(2)}, u32[]{:S(2)}) collective-permute-start(bf16[16,4096]{1,0:T(8,128)(2,1)S(1)} %get-tuple-element.35._), channel_id=1, source_target_pairs={{0,6},{1,7},{2,0},{3,1},{4,2},{5,3},{6,4},{7,5},{8,14},{9,15},{10,... | collective-permute-start | bytes 393224 | tf_op jit(solution)/shard_map/ppermute | solution.py:341
  26.7 8.6 %collective-permute-start.9 = (bf16[16,4096]{1,0:T(8,128)(2,1)S(1)}, bf16[16,4096]{1,0:T(8,128)(2,1)S(1)}, u32[]{:S(2)}, u32[]{:S(2)}) collective-permute-start(bf16[16,4096]{1,0:T(8,128)(2,1)S(1)} %shard_map.114.refs_0_), channel_id=1, source_target_pairs={{0,2},{1,3},{2,4},{3,5},{4,6},{5,7},{6,0},{7,1},{8,10},{9,11},{10,... | collective-permute-start | bytes 393224 | tf_op jit(solution)/shard_map/ppermute | solution.py:341
  30.0 9.7 %collective-permute-start.8 = (bf16[16,4096]{1,0:T(8,128)(2,1)S(1)}, bf16[16,4096]{1,0:T(8,128)(2,1)S(1)}, u32[]{:S(2)}, u32[]{:S(2)}) collective-permute-start(bf16[16,4096]{1,0:T(8,128)(2,1)S(1)} %shard_map.114.refs_0_), channel_id=1, source_target_pairs={{0,4},{1,5},{2,6},{3,7},{4,0},{5,1},{6,2},{7,3},{8,12},{9,13},{10,... | collective-permute-start | bytes 393224 | tf_op jit(solution)/shard_map/ppermute | solution.py:341
  31.6 8.1 %collective-permute-start.7 = (bf16[16,4096]{1,0:T(8,128)(2,1)S(1)}, bf16[16,4096]{1,0:T(8,128)(2,1)S(1)}, u32[]{:S(2)}, u32[]{:S(2)}) collective-permute-start(bf16[16,4096]{1,0:T(8,128)(2,1)S(1)} %shard_map.114.refs_0_), channel_id=1, source_target_pairs={{0,6},{1,7},{2,0},{3,1},{4,2},{5,3},{6,4},{7,5},{8,14},{9,15},{10,... | collective-permute-start | bytes 393224 | tf_op jit(solution)/shard_map/ppermute | solution.py:341
  32.4 7.8 %collective-permute-start.10 = (bf16[16,4096]{1,0:T(8,128)(2,1)S(1)}, bf16[16,4096]{1,0:T(8,128)(2,1)S(1)}, u32[]{:S(2)}, u32[]{:S(2)}) collective-permute-start(bf16[16,4096]{1,0:T(8,128)(2,1)S(1)} %shard_map.114.refs_0_), channel_id=1, source_target_pairs={{0,1},{1,0},{2,3},{3,2},{4,5},{5,4},{6,7},{7,6},{8,9},{9,8},{10,11... | collective-permute-start | bytes 393224 | tf_op jit(solution)/shard_map/ppermute | solution.py:344
  35.2 5.0 %collective-permute-start.13 = (bf16[16,4096]{1,0:T(8,128)(2,1)S(1)}, bf16[16,4096]{1,0:T(8,128)(2,1)S(1)}, u32[]{:S(2)}, u32[]{:S(2)}) collective-permute-start(bf16[16,4096]{1,0:T(8,128)(2,1)S(1)} %collective-permute-done.9.refs_3_), channel_id=1, source_target_pairs={{0,1},{1,0},{2,3},{3,2},{4,5},{5,4},{6,7},{7,6},{8,9},{9,8},{10,11... | collective-permute-start | bytes 393224 | tf_op jit(solution)/shard_map/ppermute | solution.py:344
  39.7 1.3 %collective-permute-start.12 = (bf16[16,4096]{1,0:T(8,128)(2,1)S(1)}, bf16[16,4096]{1,0:T(8,128)(2,1)S(1)}, u32[]{:S(2)}, u32[]{:S(2)}) collective-permute-start(bf16[16,4096]{1,0:T(8,128)(2,1)S(1)} %collective-permute-done.8.refs_2_), channel_id=1, source_target_pairs={{0,1},{1,0},{2,3},{3,2},{4,5},{5,4},{6,7},{7,6},{8,9},{9,8},{10,11... | collective-permute-start | bytes 393224 | tf_op jit(solution)/shard_map/ppermute | solution.py:344
  39.7 1.5 %collective-permute-start.11 = (bf16[16,4096]{1,0:T(8,128)(2,1)S(1)}, bf16[16,4096]{1,0:T(8,128)(2,1)S(1)}, u32[]{:S(2)}, u32[]{:S(2)}) collective-permute-start(bf16[16,4096]{1,0:T(8,128)(2,1)S(1)} %collective-permute-done.7.refs_1_), channel_id=1, source_target_pairs={{0,1},{1,0},{2,3},{3,2},{4,5},{5,4},{6,7},{7,6},{8,9},{9,8},{10,11... | collective-permute-start | bytes 393224 | tf_op jit(solution)/shard_map/ppermute | solution.py:344
  44.5 2.0 %collective-permute-start.14 = (bf16[64,4096]{1,0:T(8,128)(2,1)S(1)}, bf16[64,4096]{1,0:T(8,128)(2,1)S(1)}, u32[]{:S(2)}, u32[]{:S(2)}) collective-permute-start(bf16[64,4096]{1,0:T(8,128)(2,1)S(1)} %get-tuple-element.40), channel_id=1, source_target_pairs={{0,1},{1,0},{2,3},{3,2},{4,5},{5,4},{6,7},{7,6},{8,9},{9,8},{10,11... | collective-permute-start | bytes 1572872 | tf_op jit(solution)/shard_map/ppermute | solution.py:344
  46.6 9.1 %collective-permute-start.15 = (bf16[16,4096]{1,0:T(8,128)(2,1)S(1)}, bf16[16,4096]{1,0:T(8,128)(2,1)S(1)}, u32[]{:S(2)}, u32[]{:S(2)}) collective-permute-start(bf16[16,4096]{1,0:T(8,128)(2,1)S(1)} %get-tuple-element.42), channel_id=1, source_target_pairs={{0,2},{1,3},{2,4},{3,5},{4,6},{5,7},{6,0},{7,1},{8,10},{9,11},{10,... | collective-permute-start | bytes 393224 | tf_op jit(solution)/shard_map/ppermute | solution.py:341
  49.7 11.3 %collective-permute-start.16 = (bf16[16,4096]{1,0:T(8,128)(2,1)S(1)}, bf16[16,4096]{1,0:T(8,128)(2,1)S(1)}, u32[]{:S(2)}, u32[]{:S(2)}) collective-permute-start(bf16[16,4096]{1,0:T(8,128)(2,1)S(1)} %get-tuple-element.43), channel_id=1, source_target_pairs={{0,4},{1,5},{2,6},{3,7},{4,0},{5,1},{6,2},{7,3},{8,12},{9,13},{10,... | collective-permute-start | bytes 393224 | tf_op jit(solution)/shard_map/ppermute | solution.py:341
  51.9 9.1 %collective-permute-start.17 = (bf16[16,4096]{1,0:T(8,128)(2,1)S(1)}, bf16[16,4096]{1,0:T(8,128)(2,1)S(1)}, u32[]{:S(2)}, u32[]{:S(2)}) collective-permute-start(bf16[16,4096]{1,0:T(8,128)(2,1)S(1)} %get-tuple-element.44), channel_id=1, source_target_pairs={{0,6},{1,7},{2,0},{3,1},{4,2},{5,3},{6,4},{7,5},{8,14},{9,15},{10,... | collective-permute-start | bytes 393224 | tf_op jit(solution)/shard_map/ppermute | solution.py:341

commit v4 on v3

--- a/solution.py
+++ b/solution.py
@@ -10,7 +10,7 @@
 F32 = jnp.float32
 BF16 = jnp.bfloat16
 TILE_ROWS = 16
-COLUMNS = 1024
+COLUMNS = 512
 VMEM_LIMIT = 16 * 1024 * 1024
 
 
@@ -262,51 +262,73 @@
     exp_index = lax.axis_index("exp")
     place = place_matrix(t // (2 * n_pair), n_pair, exp_index // 2, exp_index % 2)
     normed = dot_f32(place, normed, ((1,), (0,))).astype(BF16)
-    for at in chunks(w_ref.shape[1]):
+
+    def project(at):
         part = dot_f32(normed, w_ref[:, at], ((1,), (0,))).astype(BF16)
         mine_ref[:, at] = part[: t // 2]
         theirs_ref[:, at] = part[t // 2 :]
 
-
-def chunks(width):
+    over_columns(w_ref.shape[1], project)
+
+
+def over_columns(width, body):
     size = min(width, COLUMNS)
-    return [slice(i, i + size) for i in range(0, width, size)]
+
+    def step(i, carry):
+        body(pl.ds(pl.multiple_of(i * size, size), size))
+        return carry
+
+    lax.fori_loop(0, width // size, step, 0)
 
 
 def add_kernel(groups, a_ref, b_ref, *refs):
     outs = refs[-len(groups) :]
     rows = outs[0].shape[0] // len(groups[0])
-    for group, ref in zip(groups, outs):
-        for i, block in enumerate(group):
-            at = slice(block * rows, (block + 1) * rows)
-            total = a_ref[at, :].astype(F32) + b_ref[at, :].astype(F32)
-            ref[i * rows : (i + 1) * rows, :] = total.astype(ref.dtype)
+
+    def add(at):
+        for group, ref in zip(groups, outs):
+            for i, block in enumerate(group):
+                some = slice(block * rows, (block + 1) * rows)
+                total = a_ref[some, at].astype(F32) + b_ref[some, at].astype(F32)
+                ref[i * rows : (i + 1) * rows, at] = total.astype(ref.dtype)
+
+    over_columns(a_ref.shape[1], add)
 
 
 def sum_kernel(count, *refs):
-    total = refs[0][...].astype(F32)
-    for ref in refs[1:count]:
-        total = total + ref[...].astype(F32)
-    refs[-1][...] = total.astype(BF16)
+    def add(at):
+        total = refs[0][:, at].astype(F32)
+        for ref in refs[1:count]:
+            total = total + ref[:, at].astype(F32)
+        refs[-1][:, at] = total.astype(BF16)
+
+    over_columns(refs[0].shape[1], add)
 
 
 def expert_kernel(slices, experts, count, in_ref, down_ref, member_ref, *refs):
-    parts, (mine_ref, theirs_ref) = refs[:count], refs[-2:]
+    parts, (mine_ref, theirs_ref, total_ref) = refs[:count], refs[-3:]
     hid, width = down_ref.shape
     t = member_ref.shape[1]
-    total = jnp.zeros((in_ref.shape[0], t), F32)
-    for at in chunks(width):
+    total_ref[...] = jnp.zeros(total_ref.shape, F32)
+
+    def enter(at):
         x = jnp.concatenate([part[:, at] for part in parts], axis=0)
-        total = total + dot_f32(in_ref[:, at], x, ((1,), (1,)))
-    gate, up, logits = total[0:hid], total[hid : 2 * hid], total[2 * hid : 2 * hid + experts]
+        total_ref[...] += dot_f32(in_ref[:, at], x, ((1,), (1,)))
+
+    over_columns(width, enter)
+    gate, up, logits = total_ref[0:hid], total_ref[hid : 2 * hid], total_ref[2 * hid : 2 * hid + experts]
     raised = jnp.where(member_ref[0:experts, :] > 0.5, jnp.exp(logits), 0.0)
     mine = iota2((experts, t), 0) == lax.axis_index("exp") // slices
     prob = jnp.sum(jnp.where(mine, raised, 0.0), axis=0, keepdims=True) / jnp.sum(raised, axis=0, keepdims=True)
     hidden = (gate / (1.0 + jnp.exp(-gate)) * up * prob).astype(BF16)
-    for at in chunks(width):
-        part = dot_f32(hidden, down_ref[:, at], ((0,), (0,))).astype(BF16)
+    hidden = hidden.T
+
+    def leave(at):
+        part = dot_f32(hidden, down_ref[:, at], ((1,), (0,))).astype(BF16)
         mine_ref[:, at] = part[: t // 2]
         theirs_ref[:, at] = part[t // 2 :]
+
+    over_columns(width, leave)
 
 
 def call(kernel, outs, args, scratch=(), flops=0, far=0):
@@ -356,7 +378,7 @@
         [block, block, decay_block, dma((3,))],
         far=3,
     )
-    moves = [lambda i, k=k: i ^ k for k in reversed(range(1, seq_count))]
+    moves = [lambda i, k=k: i ^ k for k in range(1, seq_count)]
     states = [lax.ppermute(state, "seq", [(move(i), i) for i in range(seq_count)]) for move in moves]
     intra, grown, query_near, gain, w_out_near = call(
         within_kernel,
@@ -400,6 +422,7 @@
             functools.partial(expert_kernel, slices, experts, 2 * len(group)),
             [rows_of(len(group))] * 2,
             (w_in, w_down_near, member, *near, *[across(x) for x in near], *parts),
+            [pltpu.VMEM((2 * hid + TILE_ROWS, 2 * len(group) * rows), F32)],
             flops=6 * 2 * len(group) * rows * hid * width,
         )
         parts = call(

time: 62.4 us -> 64 us (1.026)
  Pallas kernels: 10.7 us -> 13.2 us
  waiting for transfers between devices: 28.6 us -> 27.6 us
    pallas_call x9, Pallas kernels: 10.7 us -> 13.2 us  [call(): pl.pallas_call(kernel, out_shape=outs, in_specs=[pl.BlockSpec(memory_spac...]
    ppermute x3, waiting for transfers between devices: 3.45 us -> 2.44 us  [local(): lax.ppermute(state, 'seq', [(move(i), i) for i in range(seq_count)])]
where the time goes in v4:
time: 64 us; the launch traced here: 63.4 us
  waiting for transfers between devices  27.6 us (43%)
  starting transfers between devices  22.5 us (35%)
  Pallas kernels  13.2 us (21%)
    ppermute x9, waiting for transfers between devices, shift(): lax.ppermute(x, 'exp', [(e, (e + 2 * r) % exp_count) for e in range(exp_c...  20.6 us
    ppermute x9, starting transfers between devices, shift(): lax.ppermute(x, 'exp', [(e, (e + 2 * r) % exp_count) for e in range(exp_c...  16.9 us
    pallas_call x9, Pallas kernels, call(): pl.pallas_call(kernel, out_shape=outs, in_specs=[pl.BlockSpec(memory_spac...  13.2 us
    ppermute x3, starting transfers between devices, local(): lax.ppermute(state, 'seq', [(move(i), i) for i in range(seq_count)])  4.6 us
    ppermute x6, waiting for transfers between devices, across(): return lax.ppermute(x, 'exp', [(e, e ^ 1) for e in range(exp_count)])  4.49 us
    ppermute x3, waiting for transfers between devices, local(): lax.ppermute(state, 'seq', [(move(i), i) for i in range(seq_count)])  2.44 us
  transfers between devices with their start and end apart: 18, of which 11 were waited for; matrix products, arithmetic and copies ran while one was open for 0% of the time, Pallas kernels for 7%

profile of v4, /device:TPU:0, one launch (start us, length us, event | category | flops | bytes accessed | tf_op | source)
XLA Modules:
  0.0 63.4 jit_solution(15608202111102997341)
XLA Ops:
  0.0 1.1 %shard_map.109._ = bf16[144,128]{1,0:T(8,128)(2,1)S(1)} custom-call(bf16[128,128]{1,0:T(8,128)(2,1)} %key_hbm.3, bf16[128,128]{1,0:T(8,128)(2,1)} %value_hbm.3, f32[1,128]{1,0:T(1,128)} %bitcast.15), custom_call_target="tpu_custom_call" | custom-call | tf_op jit(solution)/shard_map/pallas_call | solution.py:339
  1.1 4.0 %collective-permute-start.2 = (bf16[144,128]{1,0:T(8,128)(2,1)S(1)}, bf16[144,128]{1,0:T(8,128)(2,1)S(1)}, u32[]{:S(2)}, u32[]{:S(2)}) collective-permute-start(bf16[144,128]{1,0:T(8,128)(2,1)S(1)} %shard_map.109._), channel_id=1, source_target_pairs={{24,0},{16,8},{8,16},{0,24},{25,1},{17,9},{9,17},{1,25},{26,2},{18... | collective-permute-start | bytes 110600 | tf_op jit(solution)/shard_map/ppermute | solution.py:382
  5.1 0.5 collective-permute-start.1
  5.6 0.1 collective-permute-start
  5.7 1.4 %shard_map.110 = (f32[128,128]{1,0:T(8,128)S(1)}, f32[128,128]{1,0:T(8,128)S(1)}, bf16[128,128]{1,0:T(8,128)(2,1)S(1)}, f32[8,128]{1,0:T(8,128)S(1)}, bf16[128,4096]{1,0:T(8,128)(2,1)S(1)}) custom-call(bf16[128,128]{1,0:T(8,128)(2,1)} %query_hbm.1, bf16[128,128]{1,0:T(8,128)(2,1)} %key_hbm.3, bf16[128,128]{1,0:T(8,128)(2,1)} %value_hbm.3, ...), custom_call_target="tpu_custom_call" | custom-call | tf_op jit(solution)/shard_map/pallas_call | solution.py:339
  7.1 0.0 collective-permute-done.2.refs_2_
  7.1 1.9 %collective-permute-done.1.refs_1_ = bf16[144,128]{1,0:T(8,128)(2,1)S(1)} collective-permute-done((bf16[144,128]{1,0:T(8,128)(2,1)S(1)}, bf16[144,128]{1,0:T(8,128)(2,1)S(1)}, u32[]{:S(2)}, u32[]{:S(2)}) %collective-permute-start.1) | collective-permute-done | bytes 36896 | tf_op jit(solution)/shard_map/ppermute | solution.py:382
  9.0 0.5 collective-permute-done.refs_0_
  9.5 1.8 %shard_map.111 = (bf16[64,4096]{1,0:T(8,128)(2,1)S(1)}, bf16[64,4096]{1,0:T(8,128)(2,1)S(1)}) custom-call(bf16[144,128]{1,0:T(8,128)(2,1)S(1)} %collective-permute-done.refs_0_, bf16[144,128]{1,0:T(8,128)(2,1)S(1)} %collective-permute-done.1.refs_1_, bf16[144,128]{1,0:T(8,128)(2,1)S(1)} %collective-permute-done.2.refs_2_, ...), custom_call_target="tpu_custom_call" | custom-call | tf_op jit(solution)/shard_map/pallas_call | solution.py:339
  11.4 0.1 collective-permute-start.3
  11.5 1.9 %collective-permute-done.3.b_ref = bf16[64,4096]{1,0:T(8,128)(2,1)S(1)} collective-permute-done((bf16[64,4096]{1,0:T(8,128)(2,1)S(1)}, bf16[64,4096]{1,0:T(8,128)(2,1)S(1)}, u32[]{:S(2)}, u32[]{:S(2)}) %collective-permute-start.3) | collective-permute-done | bytes 524320 | tf_op jit(solution)/shard_map/ppermute | solution.py:366
  13.3 0.2 shard_map.112
  13.5 1.6 %collective-permute-start.4 = (bf16[16,4096]{1,0:T(8,128)(2,1)S(1)}, bf16[16,4096]{1,0:T(8,128)(2,1)S(1)}, u32[]{:S(2)}, u32[]{:S(2)}) collective-permute-start(bf16[16,4096]{1,0:T(8,128)(2,1)S(1)} %get-tuple-element.33), channel_id=1, source_target_pairs={{0,2},{1,3},{2,4},{3,5},{4,6},{5,7},{6,0},{7,1},{8,10},{9,11},{10,... | collective-permute-start | bytes 393224 | tf_op jit(solution)/shard_map/ppermute | solution.py:363
  15.1 2.6 %collective-permute-start.5 = (bf16[16,4096]{1,0:T(8,128)(2,1)S(1)}, bf16[16,4096]{1,0:T(8,128)(2,1)S(1)}, u32[]{:S(2)}, u32[]{:S(2)}) collective-permute-start(bf16[16,4096]{1,0:T(8,128)(2,1)S(1)} %get-tuple-element.34), channel_id=1, source_target_pairs={{0,4},{1,5},{2,6},{3,7},{4,0},{5,1},{6,2},{7,3},{8,12},{9,13},{10,... | collective-permute-start | bytes 393224 | tf_op jit(solution)/shard_map/ppermute | solution.py:363
  17.7 1.3 %collective-permute-start.6 = (bf16[16,4096]{1,0:T(8,128)(2,1)S(1)}, bf16[16,4096]{1,0:T(8,128)(2,1)S(1)}, u32[]{:S(2)}, u32[]{:S(2)}) collective-permute-start(bf16[16,4096]{1,0:T(8,128)(2,1)S(1)} %get-tuple-element.35._), channel_id=1, source_target_pairs={{0,6},{1,7},{2,0},{3,1},{4,2},{5,3},{6,4},{7,5},{8,14},{9,15},{10,... | collective-permute-start | bytes 393224 | tf_op jit(solution)/shard_map/ppermute | solution.py:363
  19.1 3.2 %shard_map.113 = (bf16[592,4096]{1,0:T(8,128)(2,1)S(1)}, bf16[288,4096]{1,0:T(8,128)(2,1)S(1)}, f32[8,128]{1,0:T(8,128)S(1)}) custom-call(bf16[4,4096]{1,0:T(4,128)(2,1)} %bitcast.14, s32[2,128]{1,0:T(2,128)} %bitcast.17, bf16[288,4096]{1,0:T(8,128)(2,1)} %bitcast.11, bf16[288,4096]{1,0:T(8,128)(2,1)} %bitcast.12, bf16[288,4096]{1,0:T(8,128)(2,1)} %bitcast.13, ...), custom_call_target="tpu_custom_call" | custom-call | tf_op jit(solution)/shard_map/pallas_call | solution.py:339
  22.3 0.0 collective-permute-done.4.refs_1_
  22.3 4.4 %collective-permute-done.5.refs_2_ = bf16[16,4096]{1,0:T(8,128)(2,1)S(1)} collective-permute-done((bf16[16,4096]{1,0:T(8,128)(2,1)S(1)}, bf16[16,4096]{1,0:T(8,128)(2,1)S(1)}, u32[]{:S(2)}, u32[]{:S(2)}) %collective-permute-start.5) | collective-permute-done | bytes 131104 | tf_op jit(solution)/shard_map/ppermute | solution.py:363
  26.7 0.0 collective-permute-done.6.refs_3_
  26.7 0.1 shard_map.114.refs_0_
  26.8 3.3 %collective-permute-start.9 = (bf16[16,4096]{1,0:T(8,128)(2,1)S(1)}, bf16[16,4096]{1,0:T(8,128)(2,1)S(1)}, u32[]{:S(2)}, u32[]{:S(2)}) collective-permute-start(bf16[16,4096]{1,0:T(8,128)(2,1)S(1)} %shard_map.114.refs_0_), channel_id=1, source_target_pairs={{0,2},{1,3},{2,4},{3,5},{4,6},{5,7},{6,0},{7,1},{8,10},{9,11},{10,... | collective-permute-start | bytes 393224 | tf_op jit(solution)/shard_map/ppermute | solution.py:363
  30.1 1.6 %collective-permute-start.8 = (bf16[16,4096]{1,0:T(8,128)(2,1)S(1)}, bf16[16,4096]{1,0:T(8,128)(2,1)S(1)}, u32[]{:S(2)}, u32[]{:S(2)}) collective-permute-start(bf16[16,4096]{1,0:T(8,128)(2,1)S(1)} %shard_map.114.refs_0_), channel_id=1, source_target_pairs={{0,4},{1,5},{2,6},{3,7},{4,0},{5,1},{6,2},{7,3},{8,12},{9,13},{10,... | collective-permute-start | bytes 393224 | tf_op jit(solution)/shard_map/ppermute | solution.py:363
  31.8 0.8 %collective-permute-start.7 = (bf16[16,4096]{1,0:T(8,128)(2,1)S(1)}, bf16[16,4096]{1,0:T(8,128)(2,1)S(1)}, u32[]{:S(2)}, u32[]{:S(2)}) collective-permute-start(bf16[16,4096]{1,0:T(8,128)(2,1)S(1)} %shard_map.114.refs_0_), channel_id=1, source_target_pairs={{0,6},{1,7},{2,0},{3,1},{4,2},{5,3},{6,4},{7,5},{8,14},{9,15},{10,... | collective-permute-start | bytes 393224 | tf_op jit(solution)/shard_map/ppermute | solution.py:363
  32.6 0.0 collective-permute-start.10
  32.6 2.8 %collective-permute-done.9.refs_3_ = bf16[16,4096]{1,0:T(8,128)(2,1)S(1)} collective-permute-done((bf16[16,4096]{1,0:T(8,128)(2,1)S(1)}, bf16[16,4096]{1,0:T(8,128)(2,1)S(1)}, u32[]{:S(2)}, u32[]{:S(2)}) %collective-permute-start.9) | collective-permute-done | bytes 131104 | tf_op jit(solution)/shard_map/ppermute | solution.py:363
  35.4 0.0 collective-permute-start.13
  35.4 4.5 %collective-permute-done.8.refs_2_ = bf16[16,4096]{1,0:T(8,128)(2,1)S(1)} collective-permute-done((bf16[16,4096]{1,0:T(8,128)(2,1)S(1)}, bf16[16,4096]{1,0:T(8,128)(2,1)S(1)}, u32[]{:S(2)}, u32[]{:S(2)}) %collective-permute-start.8) | collective-permute-done | bytes 131104 | tf_op jit(solution)/shard_map/ppermute | solution.py:363
  39.9 0.0 collective-permute-start.12
  39.9 0.0 collective-permute-done.7.refs_1_
  39.9 0.5 collective-permute-start.11
  40.4 0.0 collective-permute-done.10.refs_4_
  40.4 0.0 collective-permute-done.13.refs_7_
  40.4 0.8 %collective-permute-done.12.refs_6_ = bf16[16,4096]{1,0:T(8,128)(2,1)S(1)} collective-permute-done((bf16[16,4096]{1,0:T(8,128)(2,1)S(1)}, bf16[16,4096]{1,0:T(8,128)(2,1)S(1)}, u32[]{:S(2)}, u32[]{:S(2)}) %collective-permute-start.12) | collective-permute-done | bytes 131104 | tf_op jit(solution)/shard_map/ppermute | solution.py:366
  41.2 0.2 collective-permute-done.11.refs_5_
  41.4 4.5 %shard_map.115 = (bf16[64,4096]{1,0:T(8,128)(2,1)S(1)}, bf16[64,4096]{1,0:T(8,128)(2,1)S(1)}) custom-call(bf16[592,4096]{1,0:T(8,128)(2,1)S(1)} %get-tuple-element.37.in_ref, bf16[288,4096]{1,0:T(8,128)(2,1)S(1)} %get-tuple-element.38.down_ref, f32[8,128]{1,0:T(8,128)S(1)} %get-tuple-element.36.refs_4_.member_ref, bf16[16,4096]{1,0:T(8,128)(2,1)S(1)} %shard_map.114.refs_0_, ...), custom_call_target="tpu_custom_call" | custom-call | tf_op jit(solution)/shard_map/pallas_call | solution.py:339
  45.9 0.4 collective-permute-start.14
  46.3 1.6 %collective-permute-done.14.b_ref = bf16[64,4096]{1,0:T(8,128)(2,1)S(1)} collective-permute-done((bf16[64,4096]{1,0:T(8,128)(2,1)S(1)}, bf16[64,4096]{1,0:T(8,128)(2,1)S(1)}, u32[]{:S(2)}, u32[]{:S(2)}) %collective-permute-start.14) | collective-permute-done | bytes 524320 | tf_op jit(solution)/shard_map/ppermute | solution.py:366
  47.9 0.2 shard_map.116
  48.1 3.1 %collective-permute-start.15 = (bf16[16,4096]{1,0:T(8,128)(2,1)S(1)}, bf16[16,4096]{1,0:T(8,128)(2,1)S(1)}, u32[]{:S(2)}, u32[]{:S(2)}) collective-permute-start(bf16[16,4096]{1,0:T(8,128)(2,1)S(1)} %get-tuple-element.42), channel_id=1, source_target_pairs={{0,2},{1,3},{2,4},{3,5},{4,6},{5,7},{6,0},{7,1},{8,10},{9,11},{10,... | collective-permute-start | bytes 393224 | tf_op jit(solution)/shard_map/ppermute | solution.py:363
  51.2 2.2 %collective-permute-start.16 = (bf16[16,4096]{1,0:T(8,128)(2,1)S(1)}, bf16[16,4096]{1,0:T(8,128)(2,1)S(1)}, u32[]{:S(2)}, u32[]{:S(2)}) collective-permute-start(bf16[16,4096]{1,0:T(8,128)(2,1)S(1)} %get-tuple-element.43), channel_id=1, source_target_pairs={{0,4},{1,5},{2,6},{3,7},{4,0},{5,1},{6,2},{7,3},{8,12},{9,13},{10,... | collective-permute-start | bytes 393224 | tf_op jit(solution)/shard_map/ppermute | solution.py:363
  53.4 0.2 collective-permute-start.17
  53.7 3.5 %collective-permute-done.15.refs_2_ = bf16[16,4096]{1,0:T(8,128)(2,1)S(1)} collective-permute-done((bf16[16,4096]{1,0:T(8,128)(2,1)S(1)}, bf16[16,4096]{1,0:T(8,128)(2,1)S(1)}, u32[]{:S(2)}, u32[]{:S(2)}) %collective-permute-start.15) | collective-permute-done | bytes 131104 | tf_op jit(solution)/shard_map/ppermute | solution.py:363
  57.2 5.3 %collective-permute-done.16.refs_3_ = bf16[16,4096]{1,0:T(8,128)(2,1)S(1)} collective-permute-done((bf16[16,4096]{1,0:T(8,128)(2,1)S(1)}, bf16[16,4096]{1,0:T(8,128)(2,1)S(1)}, u32[]{:S(2)}, u32[]{:S(2)}) %collective-permute-start.16) | collective-permute-done | bytes 131104 | tf_op jit(solution)/shard_map/ppermute | solution.py:363
  62.6 0.0 collective-permute-done.17.refs_4_
  62.6 0.8 %shard_map.117 = bf16[16,4096]{1,0:T(8,128)(2,1)} custom-call(bf16[16,4096]{1,0:T(8,128)(2,1)S(1)} %shard_map.114.refs_0_, bf16[16,4096]{1,0:T(8,128)(2,1)S(1)} %get-tuple-element.41.refs_1_, bf16[16,4096]{1,0:T(8,128)(2,1)S(1)} %collective-permute-done.15.refs_2_, bf16[16,4096]{1,0:T(8,128)(2,1)S(1)} %collective-permute-done.16.refs_3_, ...), custom_call_target="tpu_custom_call" | custom-call | tf_op jit(solution)/shard_map/pallas_call | solution.py:339
Async XLA Ops:
  1.1 6.0 %collective-permute-start.2 = (bf16[144,128]{1,0:T(8,128)(2,1)S(1)}, bf16[144,128]{1,0:T(8,128)(2,1)S(1)}, u32[]{:S(2)}, u32[]{:S(2)}) collective-permute-start(bf16[144,128]{1,0:T(8,128)(2,1)S(1)} %shard_map.109._), channel_id=1, source_target_pairs={{24,0},{16,8},{8,16},{0,24},{25,1},{17,9},{9,17},{1,25},{26,2},{18... | collective-permute-start | bytes 110600 | tf_op jit(solution)/shard_map/ppermute | solution.py:382
  5.1 4.0 %collective-permute-start.1 = (bf16[144,128]{1,0:T(8,128)(2,1)S(1)}, bf16[144,128]{1,0:T(8,128)(2,1)S(1)}, u32[]{:S(2)}, u32[]{:S(2)}) collective-permute-start(bf16[144,128]{1,0:T(8,128)(2,1)S(1)} %shard_map.109._), channel_id=1, source_target_pairs={{16,0},{24,8},{0,16},{8,24},{17,1},{25,9},{1,17},{9,25},{18,2},{26... | collective-permute-start | bytes 110600 | tf_op jit(solution)/shard_map/ppermute | solution.py:382
  5.6 4.0 %collective-permute-start = (bf16[144,128]{1,0:T(8,128)(2,1)S(1)}, bf16[144,128]{1,0:T(8,128)(2,1)S(1)}, u32[]{:S(2)}, u32[]{:S(2)}) collective-permute-start(bf16[144,128]{1,0:T(8,128)(2,1)S(1)} %shard_map.109._), channel_id=1, source_target_pairs={{8,0},{0,8},{24,16},{16,24},{9,1},{1,9},{25,17},{17,25},{10,2},{2,... | collective-permute-start | bytes 110600 | tf_op jit(solution)/shard_map/ppermute | solution.py:382
  11.4 2.0 %collective-permute-start.3 = (bf16[64,4096]{1,0:T(8,128)(2,1)S(1)}, bf16[64,4096]{1,0:T(8,128)(2,1)S(1)}, u32[]{:S(2)}, u32[]{:S(2)}) collective-permute-start(bf16[64,4096]{1,0:T(8,128)(2,1)S(1)} %get-tuple-element.31), channel_id=1, source_target_pairs={{0,1},{1,0},{2,3},{3,2},{4,5},{5,4},{6,7},{7,6},{8,9},{9,8},{10,11... | collective-permute-start | bytes 1572872 | tf_op jit(solution)/shard_map/ppermute | solution.py:366
  13.5 8.7 %collective-permute-start.4 = (bf16[16,4096]{1,0:T(8,128)(2,1)S(1)}, bf16[16,4096]{1,0:T(8,128)(2,1)S(1)}, u32[]{:S(2)}, u32[]{:S(2)}) collective-permute-start(bf16[16,4096]{1,0:T(8,128)(2,1)S(1)} %get-tuple-element.33), channel_id=1, source_target_pairs={{0,2},{1,3},{2,4},{3,5},{4,6},{5,7},{6,0},{7,1},{8,10},{9,11},{10,... | collective-permute-start | bytes 393224 | tf_op jit(solution)/shard_map/ppermute | solution.py:363
  15.1 11.5 %collective-permute-start.5 = (bf16[16,4096]{1,0:T(8,128)(2,1)S(1)}, bf16[16,4096]{1,0:T(8,128)(2,1)S(1)}, u32[]{:S(2)}, u32[]{:S(2)}) collective-permute-start(bf16[16,4096]{1,0:T(8,128)(2,1)S(1)} %get-tuple-element.34), channel_id=1, source_target_pairs={{0,4},{1,5},{2,6},{3,7},{4,0},{5,1},{6,2},{7,3},{8,12},{9,13},{10,... | collective-permute-start | bytes 393224 | tf_op jit(solution)/shard_map/ppermute | solution.py:363
  17.7 8.9 %collective-permute-start.6 = (bf16[16,4096]{1,0:T(8,128)(2,1)S(1)}, bf16[16,4096]{1,0:T(8,128)(2,1)S(1)}, u32[]{:S(2)}, u32[]{:S(2)}) collective-permute-start(bf16[16,4096]{1,0:T(8,128)(2,1)S(1)} %get-tuple-element.35._), channel_id=1, source_target_pairs={{0,6},{1,7},{2,0},{3,1},{4,2},{5,3},{6,4},{7,5},{8,14},{9,15},{10,... | collective-permute-start | bytes 393224 | tf_op jit(solution)/shard_map/ppermute | solution.py:363
  26.8 8.6 %collective-permute-start.9 = (bf16[16,4096]{1,0:T(8,128)(2,1)S(1)}, bf16[16,4096]{1,0:T(8,128)(2,1)S(1)}, u32[]{:S(2)}, u32[]{:S(2)}) collective-permute-start(bf16[16,4096]{1,0:T(8,128)(2,1)S(1)} %shard_map.114.refs_0_), channel_id=1, source_target_pairs={{0,2},{1,3},{2,4},{3,5},{4,6},{5,7},{6,0},{7,1},{8,10},{9,11},{10,... | collective-permute-start | bytes 393224 | tf_op jit(solution)/shard_map/ppermute | solution.py:363
  30.1 9.7 %collective-permute-start.8 = (bf16[16,4096]{1,0:T(8,128)(2,1)S(1)}, bf16[16,4096]{1,0:T(8,128)(2,1)S(1)}, u32[]{:S(2)}, u32[]{:S(2)}) collective-permute-start(bf16[16,4096]{1,0:T(8,128)(2,1)S(1)} %shard_map.114.refs_0_), channel_id=1, source_target_pairs={{0,4},{1,5},{2,6},{3,7},{4,0},{5,1},{6,2},{7,3},{8,12},{9,13},{10,... | collective-permute-start | bytes 393224 | tf_op jit(solution)/shard_map/ppermute | solution.py:363
  31.8 8.1 %collective-permute-start.7 = (bf16[16,4096]{1,0:T(8,128)(2,1)S(1)}, bf16[16,4096]{1,0:T(8,128)(2,1)S(1)}, u32[]{:S(2)}, u32[]{:S(2)}) collective-permute-start(bf16[16,4096]{1,0:T(8,128)(2,1)S(1)} %shard_map.114.refs_0_), channel_id=1, source_target_pairs={{0,6},{1,7},{2,0},{3,1},{4,2},{5,3},{6,4},{7,5},{8,14},{9,15},{10,... | collective-permute-start | bytes 393224 | tf_op jit(solution)/shard_map/ppermute | solution.py:363
  32.6 7.8 %collective-permute-start.10 = (bf16[16,4096]{1,0:T(8,128)(2,1)S(1)}, bf16[16,4096]{1,0:T(8,128)(2,1)S(1)}, u32[]{:S(2)}, u32[]{:S(2)}) collective-permute-start(bf16[16,4096]{1,0:T(8,128)(2,1)S(1)} %shard_map.114.refs_0_), channel_id=1, source_target_pairs={{0,1},{1,0},{2,3},{3,2},{4,5},{5,4},{6,7},{7,6},{8,9},{9,8},{10,11... | collective-permute-start | bytes 393224 | tf_op jit(solution)/shard_map/ppermute | solution.py:366
  35.4 5.0 %collective-permute-start.13 = (bf16[16,4096]{1,0:T(8,128)(2,1)S(1)}, bf16[16,4096]{1,0:T(8,128)(2,1)S(1)}, u32[]{:S(2)}, u32[]{:S(2)}) collective-permute-start(bf16[16,4096]{1,0:T(8,128)(2,1)S(1)} %collective-permute-done.9.refs_3_), channel_id=1, source_target_pairs={{0,1},{1,0},{2,3},{3,2},{4,5},{5,4},{6,7},{7,6},{8,9},{9,8},{10,11... | collective-permute-start | bytes 393224 | tf_op jit(solution)/shard_map/ppermute | solution.py:366
  39.9 1.3 %collective-permute-start.12 = (bf16[16,4096]{1,0:T(8,128)(2,1)S(1)}, bf16[16,4096]{1,0:T(8,128)(2,1)S(1)}, u32[]{:S(2)}, u32[]{:S(2)}) collective-permute-start(bf16[16,4096]{1,0:T(8,128)(2,1)S(1)} %collective-permute-done.8.refs_2_), channel_id=1, source_target_pairs={{0,1},{1,0},{2,3},{3,2},{4,5},{5,4},{6,7},{7,6},{8,9},{9,8},{10,11... | collective-permute-start | bytes 393224 | tf_op jit(solution)/shard_map/ppermute | solution.py:366
  39.9 1.5 %collective-permute-start.11 = (bf16[16,4096]{1,0:T(8,128)(2,1)S(1)}, bf16[16,4096]{1,0:T(8,128)(2,1)S(1)}, u32[]{:S(2)}, u32[]{:S(2)}) collective-permute-start(bf16[16,4096]{1,0:T(8,128)(2,1)S(1)} %collective-permute-done.7.refs_1_), channel_id=1, source_target_pairs={{0,1},{1,0},{2,3},{3,2},{4,5},{5,4},{6,7},{7,6},{8,9},{9,8},{10,11... | collective-permute-start | bytes 393224 | tf_op jit(solution)/shard_map/ppermute | solution.py:366
  45.9 2.0 %collective-permute-start.14 = (bf16[64,4096]{1,0:T(8,128)(2,1)S(1)}, bf16[64,4096]{1,0:T(8,128)(2,1)S(1)}, u32[]{:S(2)}, u32[]{:S(2)}) collective-permute-start(bf16[64,4096]{1,0:T(8,128)(2,1)S(1)} %get-tuple-element.40), channel_id=1, source_target_pairs={{0,1},{1,0},{2,3},{3,2},{4,5},{5,4},{6,7},{7,6},{8,9},{9,8},{10,11... | collective-permute-start | bytes 1572872 | tf_op jit(solution)/shard_map/ppermute | solution.py:366
  48.1 9.1 %collective-permute-start.15 = (bf16[16,4096]{1,0:T(8,128)(2,1)S(1)}, bf16[16,4096]{1,0:T(8,128)(2,1)S(1)}, u32[]{:S(2)}, u32[]{:S(2)}) collective-permute-start(bf16[16,4096]{1,0:T(8,128)(2,1)S(1)} %get-tuple-element.42), channel_id=1, source_target_pairs={{0,2},{1,3},{2,4},{3,5},{4,6},{5,7},{6,0},{7,1},{8,10},{9,11},{10,... | collective-permute-start | bytes 393224 | tf_op jit(solution)/shard_map/ppermute | solution.py:363
  51.2 11.3 %collective-permute-start.16 = (bf16[16,4096]{1,0:T(8,128)(2,1)S(1)}, bf16[16,4096]{1,0:T(8,128)(2,1)S(1)}, u32[]{:S(2)}, u32[]{:S(2)}) collective-permute-start(bf16[16,4096]{1,0:T(8,128)(2,1)S(1)} %get-tuple-element.43), channel_id=1, source_target_pairs={{0,4},{1,5},{2,6},{3,7},{4,0},{5,1},{6,2},{7,3},{8,12},{9,13},{10,... | collective-permute-start | bytes 393224 | tf_op jit(solution)/shard_map/ppermute | solution.py:363
  53.4 9.1 %collective-permute-start.17 = (bf16[16,4096]{1,0:T(8,128)(2,1)S(1)}, bf16[16,4096]{1,0:T(8,128)(2,1)S(1)}, u32[]{:S(2)}, u32[]{:S(2)}) collective-permute-start(bf16[16,4096]{1,0:T(8,128)(2,1)S(1)} %get-tuple-element.44), channel_id=1, source_target_pairs={{0,6},{1,7},{2,0},{3,1},{4,2},{5,3},{6,4},{7,5},{8,14},{9,15},{10,... | collective-permute-start | bytes 393224 | tf_op jit(solution)/shard_map/ppermute | solution.py:363
